TPU v7x, 128 devices: a whole 4x4x4 slice. The times are simulated.
128 devices in a mesh: section: 2 (over z_lo), peer: 64 (over x, y, z_hi, core).
Axes of the slice: x: 4, y: 4, z: 4 (z_hi: 2, z_lo: 2; z = z_hi * 2 + z_lo), core: 2. Of those that a mesh axis runs over, the one named last changes fastest.
Arguments:
- batch_ends: bfloat16 [2, 8192, 5120], P('section', 'peer'), may hold values from -6 to 6
- wiring: int32 [64], replicated, may hold values from 0 to 63, as said below
- down_proj: bfloat16 [2, 64, 5120, 256], P('section', 'peer'), may hold values from -0.078125 to 0.078125
- up_proj: bfloat16 [2, 64, 256, 5120], P('section', 'peer'), may hold values from -0.375 to 0.375
- norm_gain: bfloat16 [2, 64, 5120], P('section', 'peer'), may hold values from 0.099609375 to 1.8984375
Outputs:
- ends_grad: bfloat16 [2, 8192, 5120], P('section', 'peer')
- down_grad: float32 [2, 5120, 256], P('section', 'peer')
- up_grad: float32 [2, 256, 5120], P('section', 'peer')
Inputs may be any that keep to these rules, and one draw needn't show every extreme that they name: `wiring`: no value is named by more than 2 entries; a quarter of the peers are named by exactly 2 entries, half by one, a quarter by none.
All inputs are finite; a program needn't handle non-finite values.
Results may differ from a plain program's by a relative error of at most 0.0067.
Values may be sent and summed in bfloat16 or wider, within the bound.
A program may use at most 128 MiB of HBM per device.

v0:
```python
import math

import jax
import jax.numpy as jnp
from jax import lax
from jax.sharding import PartitionSpec as P

CAP = 2


def shifted(block, axis, distance):
    devices = range(lax.axis_size(axis))
    route = [((i - distance) % len(devices), i) for i in devices]
    return lax.ppermute(block, axis, route)


def contract_rows(left, right):
    return lax.dot_general(
        left, right, (((0,), (0,)), ((), ())), preferred_element_type=jnp.float32
    )


def contract_cols(left, right):
    return lax.dot_general(
        left, right, (((1,), (1,)), ((), ())), preferred_element_type=jnp.float32
    )


def section_forward(tok_rows, norm_scale, down_matrix, up_matrix):
    values = tok_rows.astype(jnp.float32)
    inverse = lax.rsqrt(jnp.mean(values * values, axis=-1, keepdims=True) + 1e-06)
    normed = (values * inverse * norm_scale.astype(jnp.float32)).astype(jnp.bfloat16)
    activation = jnp.dot(normed, down_matrix, preferred_element_type=jnp.float32)
    squashed = jax.nn.silu(activation).astype(jnp.bfloat16)
    result = (values + jnp.dot(squashed, up_matrix, preferred_element_type=jnp.float32)).astype(
        jnp.bfloat16
    )
    return (result, (normed, activation, squashed, inverse))


def section_backward(tok_rows, cotangent, norm_scale, down_matrix, up_matrix, saved):
    normed, activation, squashed, inverse = saved
    grad_up = contract_rows(squashed, cotangent)
    grad_squash = contract_cols(cotangent, up_matrix)
    sigmoid = jax.nn.sigmoid(activation)
    grad_act = (grad_squash * sigmoid * (1.0 + activation * (1.0 - sigmoid))).astype(jnp.bfloat16)
    grad_down = contract_rows(normed, grad_act)
    grad_normed = contract_cols(grad_act, down_matrix) * norm_scale.astype(jnp.float32)
    values = tok_rows.astype(jnp.float32)
    grad_values = inverse * grad_normed - values * inverse**3 * jnp.mean(
        values * grad_normed, axis=-1, keepdims=True
    )
    grad_rows = (cotangent.astype(jnp.float32) + grad_values).astype(jnp.bfloat16)
    return (grad_rows, grad_down, grad_up)


def exchange_blocks(pieces):
    return lax.all_to_all(pieces, "peer", split_axis=2, concat_axis=2, tiled=True)


def cross_section(payload):
    return shifted(payload, "section", 1)


def deliver(items, table, peers):
    count, tok_count, width = items.shape
    block_rows = tok_count // peers
    spread = exchange_blocks(items.reshape(count, 1, peers, block_rows * width))
    placed = jnp.einsum(
        "kqs,msf->mkqf", table, spread[:, 0], preferred_element_type=jnp.float32
    ).astype(jnp.bfloat16)
    arrived = exchange_blocks(placed)
    return arrived.reshape(count, table.shape[0], tok_count, width)


def withdraw(items, table, peers):
    count, capacity, tok_count, width = items.shape
    block_rows = tok_count // peers
    spread = exchange_blocks(items.reshape(count, capacity, peers, block_rows * width))
    picked = jnp.einsum("kqs,mkqf->msf", table, spread, preferred_element_type=jnp.float32).astype(
        jnp.bfloat16
    )
    arrived = exchange_blocks(picked[:, None])
    return arrived.reshape(count, tok_count, width)


def shards(batch_ends, wiring, down_proj, up_proj, norm_gain):
    peers = lax.axis_size("peer")
    is_first = lax.axis_index("section") == 0
    tok_rows = batch_ends[0]
    down_matrix = down_proj[0, 0]
    up_matrix = up_proj[0, 0]
    norm_scale = norm_gain[0, 0]
    tok_count, width = tok_rows.shape
    bottleneck = down_matrix.shape[1]
    sources = jnp.arange(peers, dtype=jnp.int32)
    same_target = wiring[:, None] == wiring[None, :]
    earlier = sources[None, :] < sources[:, None]
    slot_rank = jnp.sum((same_target & earlier).astype(jnp.int32), axis=1)
    slot_ids = jnp.arange(CAP, dtype=jnp.int32)
    table = (
        (wiring[None, None, :] == sources[None, :, None])
        & (slot_rank[None, None, :] == slot_ids[:, None, None])
    ).astype(jnp.bfloat16)

    def front_forward():
        return section_forward(tok_rows, norm_scale, down_matrix, up_matrix)

    def front_keep():
        empty_saved = (
            jnp.zeros((tok_count, width), jnp.bfloat16),
            jnp.zeros((tok_count, bottleneck), jnp.float32),
            jnp.zeros((tok_count, bottleneck), jnp.bfloat16),
            jnp.zeros((tok_count, 1), jnp.float32),
        )
        return (tok_rows, empty_saved)

    outgoing, saved_front = lax.cond(is_first, front_forward, front_keep)
    crossed = cross_section(outgoing)
    routed = deliver(jnp.stack([crossed, tok_rows]), table, peers)
    inbound = routed[0]
    cot_slots = routed[1]
    slot_rows = CAP * tok_count

    def later_pass():
        flat_in = inbound.reshape(slot_rows, width)
        flat_cot = cot_slots.reshape(slot_rows, width)
        ignored, saved_later = section_forward(flat_in, norm_scale, down_matrix, up_matrix)
        return section_backward(flat_in, flat_cot, norm_scale, down_matrix, up_matrix, saved_later)

    def later_skip():
        return (
            jnp.zeros((slot_rows, width), jnp.bfloat16),
            jnp.zeros((width, bottleneck), jnp.float32),
            jnp.zeros((bottleneck, width), jnp.float32),
        )

    back_rows, later_down, later_up = lax.cond(is_first, later_skip, later_pass)
    returned = withdraw(back_rows.reshape(1, CAP, tok_count, width), table, peers)[0]
    landed = cross_section(returned)

    def front_pass():
        return section_backward(tok_rows, landed, norm_scale, down_matrix, up_matrix, saved_front)

    def front_skip():
        return (
            jnp.zeros((tok_count, width), jnp.bfloat16),
            jnp.zeros((width, bottleneck), jnp.float32),
            jnp.zeros((bottleneck, width), jnp.float32),
        )

    front_rows, front_down, front_up = lax.cond(is_first, front_pass, front_skip)
    ends_block = jnp.where(is_first, front_rows, returned)[None]
    shard_down, shard_up = (
        lax.psum_scatter(front_down + later_down, "peer", scatter_dimension=0, tiled=True),
        lax.psum_scatter(front_up + later_up, "peer", scatter_dimension=0, tiled=True),
    )
    factor = 1.0 / math.sqrt(tok_count * peers)
    return (ends_block, (shard_down * factor)[None], (shard_up * factor)[None])


def solution(mesh):
    return jax.shard_map(
        shards,
        mesh=mesh,
        in_specs=(
            P("section", "peer", None),
            P(),
            P("section", "peer", None, None),
            P("section", "peer", None, None),
            P("section", "peer", None),
        ),
        out_specs=(
            P("section", "peer", None),
            P("section", "peer", None),
            P("section", "peer", None),
        ),
        check_vma=False,
    )
```

profile of v0, /device:TPU:0, one launch (start us, length us, event | category | flops | bytes accessed | tf_op | source)
XLA Modules:
  0.0 1407.8 jit_solution(15672119593176154154)
XLA Ops:
  7.2 0.8 reduce.2
  8.0 9.8 conditional.3
  8.0 0.0 copy-start.3
  8.0 1.8 fusion.1
  9.8 2.8 fusion.3
  12.6 2.7 multiply_convert_fusion
  15.2 0.0 copy-done.1
  15.3 2.5 fusion
  17.7 0.0 collective-permute-start
  17.7 1.6 stack.9
  19.3 28.5 %collective-permute-done = bf16[128,5120]{1,0:T(8,128)(2,1)} collective-permute-done((bf16[128,5120]{1,0:T(8,128)(2,1)}, bf16[128,5120]{1,0:T(8,128)(2,1)}, u32[]{:S(2)}, u32[]{:S(2)}) %collective-permute-start) | collective-permute-done | bytes 1310752 | tf_op jit(solution)/shard_map/ppermute | solution.py:14
  47.8 1.6 stack.8
  49.4 0.2 pad_maximum_fusion
  49.7 4.2 copy.17
  53.9 12.4 all-to-all-start
  66.3 0.0 copy-done.10
  66.3 0.1 convert_reduce_fusion
  66.4 0.1 iota_compare_fusion.1
  66.5 35.3 %all-to-all-done = bf16[2,1,64,10240]{3,0,1,2:T(2,128)(2,1)S(1)} async-done(((bf16[2,1,64,10240]{3,0,1,2:T(2,128)(2,1)}), bf16[2,1,64,10240]{3,0,1,2:T(2,128)(2,1)S(1)}, u32[]{:S(2)}, u32[]{:S(2)}) %all-to-all-start) | async-done | bytes 2621472 | tf_op jit(solution)/shard_map/all_to_all | solution.py:58
  101.8 3.9 fusion.21
  105.7 10.3 copy.20
  116.0 6.0 all-to-all-start.1
  122.0 0.0 all-reduce.3.cloned.1.call-start
  122.1 63.7 %all-to-all-done.1 = bf16[2,2,64,10240]{3,1,0,2:T(2,128)(2,1)} async-done(((bf16[2,2,64,10240]{3,1,0,2:T(2,128)(2,1)}), bf16[2,2,64,10240]{3,1,0,2:T(2,128)(2,1)}, u32[]{:S(2)}, u32[]{:S(2)}) %all-to-all-start.1) | async-done | bytes 5242912 | tf_op jit(solution)/shard_map/all_to_all | solution.py:58
  185.8 0.0 copy-done.2
  185.8 6.3 conditional.4
  186.2 2.6 broadcast.142
  188.8 3.0 broadcast.143
  191.8 0.3 broadcast.141
  192.1 1.5 copy-done.8
  193.6 3.0 reshape_reshape.3
  196.6 2.7 copy.22
  199.3 48.3 %all_to_all.20 = bf16[1,2,64,10240]{3,1,0,2:T(2,128)(2,1)S(1)} all-to-all(bf16[1,2,64,10240]{3,1,0,2:T(2,128)(2,1)S(1)} %copy.22), channel_id=1, replica_groups=mesh['section'=2,'peer'=64] {'peer'}, dimensions={2} | all-to-all | bytes 5242880 | tf_op jit(solution)/shard_map/all_to_all | solution.py:58
  247.6 1.1 fusion.23
  248.8 2.0 copy.40
  250.8 0.5 broadcast.171
  251.3 9.5 reduce.5
  260.8 2.1 reshape.152
  262.9 26.8 %all_to_all.21 = bf16[64,2,5120]{2,1,0:T(2,128)(2,1)S(1)} all-to-all(bf16[64,2,5120]{2,1,0:T(2,128)(2,1)S(1)} %reshape.152), channel_id=1, replica_groups=mesh['section'=2,'peer'=64] {'peer'}, dimensions={0} | all-to-all | bytes 2621440 | tf_op jit(solution)/shard_map/all_to_all | solution.py:58
  289.7 3.6 reshape.153
  293.2 9.4 bitcast_reduce_fusion
  302.6 1.4 squeeze_reshape.3
  304.0 46.8 %collective-permute-start.1 = (bf16[128,5120]{1,0:T(8,128)(2,1)}, bf16[128,5120]{1,0:T(8,128)(2,1)S(1)}, u32[]{:S(2)}, u32[]{:S(2)}) collective-permute-start(bf16[128,5120]{1,0:T(8,128)(2,1)} %squeeze_reshape.3), channel_id=1, source_target_pairs={{64,0},{0,64},{65,1},{1,65},{66,2},{2,66},{67,3},{3,67},{68,4},{4,... | collective-permute-start | bytes 3932168 | tf_op jit(solution)/shard_map/ppermute | solution.py:14
  350.8 29.3 %collective-permute-done.1 = bf16[128,5120]{1,0:T(8,128)(2,1)S(1)} collective-permute-done((bf16[128,5120]{1,0:T(8,128)(2,1)}, bf16[128,5120]{1,0:T(8,128)(2,1)S(1)}, u32[]{:S(2)}, u32[]{:S(2)}) %collective-permute-start.1) | collective-permute-done | bytes 1310752 | tf_op jit(solution)/shard_map/ppermute | solution.py:14
  380.1 20.7 %conditional.5 = (bf16[128,5120]{1,0:T(8,128)(2,1)}, f32[256,5120]{1,0:T(8,128)}, f32[5120,256]{1,0:T(8,128)}) conditional(s32[]{:T(128)} %convert_element_type.93, () %tuple.32, (bf16[128,5120]{1,0:T(8,128)(2,1)S(1)}, f32[128,1]{0,1:T(1,128)S(1)}, bf16[256,5120]{1,0:T(8,128)(2,1)}, f32[128,256]{1,0:T(8,128)S(1)}, bf16[5120,256]{1,0:T(8,128)(2,1)}, ...), branch_computations={%region_8.9_spmd, %region_9.11_spmd} | conditional | flops 1350341888 | bytes 51566644 | solution.py:152
  380.3 0.0 copy-start.4
  380.3 2.9 fusion.19
  383.2 1.1 fusion.17
  384.4 1.9 fusion.16
  386.3 4.5 convolution_bitcast_fusion
  390.8 6.0 copy.30
  396.8 4.0 fusion.36
  400.8 7.2 add.63
  408.0 0.0 all-reduce.3.cloned.1.call-update
  408.0 0.0 reduce-scatter.2.cloned.1.call-start
  408.0 7.1 add.62
  415.1 0.0 reduce-scatter.2.cloned.1.call-update
  415.2 0.6 copy-done.11
  415.8 0.6 dynamic-slice
  417.0 2.5 select_bitcast_fusion
  419.6 636.1 %all-reduce.3.cloned.1.call-done = f32[256,5120]{1,0:T(8,128)} async-done(((f32[256,5120]{1,0:T(8,128)}), f32[256,5120]{1,0:T(8,128)}) %all-reduce.3.cloned.1.call-update) | async-done | bytes 5242896
  1055.7 1.6 fusion.29
  1057.2 342.0 %reduce-scatter.2.cloned.1.call-done = f32[80,256]{1,0:T(8,128)} async-done(((f32[5120,256]{1,0:T(8,128)}), f32[80,256]{1,0:T(8,128)}) %reduce-scatter.2.cloned.1.call-update) | async-done | bytes 81936 | tf_op jit(solution)/shard_map/reduce_scatter | solution.py:155
  1399.2 1.5 multiply_bitcast_fusion
  (19 shorter events, 0.1 us)
Async XLA Ops:
  8.0 4.6 copy-start.3
  12.6 2.7 copy-start.1
  12.6 2.7 copy-start.7
  17.7 30.1 %collective-permute-start = (bf16[128,5120]{1,0:T(8,128)(2,1)}, bf16[128,5120]{1,0:T(8,128)(2,1)}, u32[]{:S(2)}, u32[]{:S(2)}) collective-permute-start(bf16[128,5120]{1,0:T(8,128)(2,1)} %get-tuple-element.71), channel_id=1, source_target_pairs={{64,0},{0,64},{65,1},{1,65},{66,2},{2,66},{67,3},{3,67},{68,4},{4,... | collective-permute-start | bytes 3932168 | tf_op jit(solution)/shard_map/ppermute | solution.py:14
  53.9 12.4 copy-start.10
  53.9 47.9 %all-to-all-start = ((bf16[2,1,64,10240]{3,0,1,2:T(2,128)(2,1)}), bf16[2,1,64,10240]{3,0,1,2:T(2,128)(2,1)S(1)}, u32[]{:S(2)}, u32[]{:S(2)}) async-start(bf16[2,1,64,10240]{3,0,1,2:T(2,128)(2,1)} %copy.17), calls=%async_computation | async-start | bytes 5242880 | tf_op jit(solution)/shard_map/all_to_all | solution.py:58
  116.0 69.8 %copy-start.2 = (bf16[1,1,5120,256]{3,2,1,0:T(8,128)(2,1)S(1)}, bf16[1,1,5120,256]{3,2,1,0:T(8,128)(2,1)}, u32[]{:S(2)}) copy-start(bf16[1,1,5120,256]{3,2,1,0:T(8,128)(2,1)} %param.13) | copy-start | bytes 7864324
  116.0 69.8 %all-to-all-start.1 = ((bf16[2,2,64,10240]{3,1,0,2:T(2,128)(2,1)}), bf16[2,2,64,10240]{3,1,0,2:T(2,128)(2,1)}, u32[]{:S(2)}, u32[]{:S(2)}) async-start(bf16[2,2,64,10240]{3,1,0,2:T(2,128)(2,1)} %copy.20), calls=%async_computation.1 | async-start | bytes 10485760 | tf_op jit(solution)/shard_map/all_to_all | solution.py:58
  122.0 933.6 %all-reduce.3.cloned.1.call-start = ((), (), s32[]{:S(2)}) async-start(), calls=%async_computation.6 | async-start | bytes 10485760
  192.1 1.5 copy-start.8
  293.2 86.8 %copy-start = (bf16[1,128,5120]{2,1,0:T(8,128)(2,1)S(1)}, bf16[1,128,5120]{2,1,0:T(8,128)(2,1)}, u32[]{:S(2)}) copy-start(bf16[1,128,5120]{2,1,0:T(8,128)(2,1)} %param.11) | copy-start | bytes 3932164
  304.0 76.1 %collective-permute-start.1 = (bf16[128,5120]{1,0:T(8,128)(2,1)}, bf16[128,5120]{1,0:T(8,128)(2,1)S(1)}, u32[]{:S(2)}, u32[]{:S(2)}) collective-permute-start(bf16[128,5120]{1,0:T(8,128)(2,1)} %squeeze_reshape.3), channel_id=1, source_target_pairs={{64,0},{0,64},{65,1},{1,65},{66,2},{2,66},{67,3},{3,67},{68,4},{4,... | collective-permute-start | bytes 3932168 | tf_op jit(solution)/shard_map/ppermute | solution.py:14
  380.3 2.9 copy-start.4
  408.0 991.2 %reduce-scatter.2.cloned.1.call-start = ((), (), s32[]{:S(2)}) async-start(), calls=%async_computation.5 | async-start | bytes 5324800 | tf_op jit(solution)/shard_map/reduce_scatter | solution.py:155
  415.1 0.7 copy-start.11
  415.1 1.9 copy-start.9
Sparse Core Ops, SparseCore 0:
  408.1 647.4 all-reduce.2
  1058.0 341.1 reduce-scatter.1
where the time goes:
time: 1410 us
  waiting for transfers between devices  1130 us (80%)
  blocking collectives  75.1 us (5%)
  starting transfers between devices  65.3 us (5%)
  local copies, waits for them, and re-layouts  56.9 us (4%)
  other arithmetic  37.1 us (3%)
  matrix products  22.7 us (2%)
  between operations  15.1 us (1%)
    unnamed x3, waiting for transfers between devices  636 us
    reduce_scatter x1, waiting for transfers between devices, shards(): lax.psum_scatter(front_down + later_down, 'peer', scatter_dimension=0, ti...  342 us
    all_to_all x2, waiting for transfers between devices, exchange_blocks(): lax.all_to_all(pieces, 'peer', split_axis=2, concat_axis=2, tiled=True)  99.1 us
    all_to_all x2, blocking collectives, exchange_blocks(): lax.all_to_all(pieces, 'peer', split_axis=2, concat_axis=2, tiled=True)  75.1 us
    ppermute x2, waiting for transfers between devices, shifted(): return lax.ppermute(block, axis, route)  57.7 us
    ppermute x2, starting transfers between devices, shifted(): return lax.ppermute(block, axis, route)  46.8 us
  transfers between devices with their start and end apart: 6, of which 6 were waited for; matrix products, arithmetic and copies ran while one was open for 1% of the time, Pallas kernels for 0%

commit v1 on v0

v1 whole, which is shorter than its diff:
```python
import functools
import math

import jax
import jax.numpy as jnp
from jax import lax
from jax.experimental import pallas as pl
from jax.experimental.pallas import tpu as pltpu
from jax.sharding import PartitionSpec as P

N = 64
ROWS = 16
COLS = 640
WAYS = 8
TOK, WIDTH, RANK = 128, 5120, 256
BF, F32 = jnp.bfloat16, jnp.float32
MESH = pl.DeviceIdType.MESH

(ENDS, COT, HID, GAIN, NORM, SQ0, BACK, SQ1, GA1, BND0, BND1, GA0, DOWN, UPA, UPA1, UPB, CLASSES) = range(17)


def target(p, k):
    a = lax.rem(lax.rem(k, 4) + 2 * lax.rem(p, 2), 4)
    b = lax.rem(k // 4, 4)
    x = lax.rem(p // 16 + a, 4)
    y = lax.rem(lax.rem(p // 4, 4) + a + b, 4)
    z = lax.rem(lax.rem(p // 2, 2) + lax.rem(k // 16, 2) + a, 2)
    core = lax.rem(lax.rem(p, 2) + k // 32 + a // 2, 2)
    return x * 16 + y * 4 + z * 2 + core


def nn(left, right):
    return jnp.dot(left, right, preferred_element_type=F32)


def nt(left, right):
    return lax.dot_general(left, right, (((1,), (1,)), ((), ())), preferred_element_type=F32)


def tn(left, right):
    return lax.dot_general(left, right, (((0,), (0,)), ((), ())), preferred_element_type=F32)


def loop(count, body):
    def step(k, carry):
        body(k)
        return carry

    lax.fori_loop(0, count, step, 0)


def tile(t):
    return pl.ds(pl.multiple_of(t * COLS, 128), COLS)


def strip(i):
    return pl.ds(pl.multiple_of(i * ROWS, ROWS), ROWS)


def step_kernel(
    from_ref, back_ref, own_ref, down_ref, up_ref, gain_ref,
    ends_ref, dgrad_ref, ugrad_ref,
    pieces, picked, hid, normed, hid_in, cot_in, gain_out, gain_in, norm_in,
    sq_out, sq0_in, sq_slots, ga_slots, back_in, sq1_in, ga1_in, bnd_pick, bnd, sq_pick,
    ga_out, ga0_in, act_ref, gsq_ref, inv_ref, part_d, part_u, part_u1, acc_d, acc_u, slab, slab_in,
    send, recv,
):
    s = lax.axis_index("section")
    p = lax.axis_index("peer")
    first, second = s == 0, s == 1
    row_group, col_group = p // WAYS, lax.rem(p, WAYS)
    my_rows, my_cols = strip(row_group), tile(col_group)

    def push(src, dst, kind, section, peer):
        pltpu.make_async_remote_copy(
            src_ref=src, dst_ref=dst, send_sem=send.at[kind], recv_sem=recv.at[kind],
            device_id={"section": section, "peer": peer}, device_id_type=MESH,
        ).start()

    def push_or_keep(src, dst, kind, peer):
        @pl.when(peer != p)
        def _():
            push(src, dst, kind, s, peer)

        @pl.when(peer == p)
        def _():
            pltpu.make_async_copy(src, dst, recv.at[kind]).start()

    def arrived(kind, ref):
        pltpu.make_async_copy(ref, ref, recv.at[kind]).wait()

    def left(kind, ref):
        pltpu.make_async_copy(ref, ref, send.at[kind]).wait()

    barrier = pltpu.get_barrier_semaphore()

    def greet(k):
        t = lax.rem(p + k, N)
        pl.semaphore_signal(barrier, inc=1, device_id={"section": 1 - s, "peer": t}, device_id_type=MESH)

        @pl.when(k > 0)
        def _():
            pl.semaphore_signal(barrier, inc=1, device_id={"section": s, "peer": t}, device_id_type=MESH)

    loop(N, greet)

    def all_here():
        pl.semaphore_wait(barrier, 2 * N - 1)

    def choose_and_send(kind, dst_ref):
        def one(k):
            q = target(p, k)
            picked[q, 0] = pieces[from_ref[0, q]]
            picked[q, 1] = pieces[from_ref[1, q]]
            dst = dst_ref.at[:, my_rows, my_cols]
            if kind == HID:
                push_or_keep(picked.at[q], dst, kind, q)
            else:
                push(picked.at[q], dst, kind, 1, q)

        loop(N, one)

    def middle(act, gsq):
        sig = jax.nn.sigmoid(act)
        squashed = (act * sig).astype(BF)
        ga = (gsq * sig * (1.0 + act * (1.0 - sig))).astype(BF)
        return squashed, ga

    def partial(out, left_ref, right_ref):
        out[...] = jnp.zeros_like(out)

        def some(t):
            rows = pl.ds(t * 16, 16)
            a = left_ref[rows].reshape(16 * ROWS, left_ref.shape[2])
            b = right_ref[rows].reshape(16 * ROWS, right_ref.shape[2])
            out[...] += tn(a, b)

        loop(4, some)

    def send_up(part, kind, section):
        def one(i):
            src = part.at[pl.ds(pl.multiple_of(i * 32, 32), 32)]
            dst = acc_u.at[row_group]
            peer = i * WAYS + col_group
            if kind == UPA:
                push_or_keep(src, dst, kind, peer)
            else:
                push(src, dst, kind, section, peer)

        loop(WAYS, one)

    def send_down():
        def one(r):
            src = part_d.at[pl.ds(pl.multiple_of(r * 80, 16), 80)]
            push_or_keep(src, acc_d.at[row_group], DOWN, col_group * WAYS + r)

        loop(WAYS, one)

    factor = 1.0 / math.sqrt(TOK * N)

    def finish_up(kind):
        arrived(kind, acc_u)
        total = acc_u[0]
        for i in range(1, WAYS):
            total = total + acc_u[i]
        total = total * factor
        for r in range(WAYS):
            slab[r, 0:4, :] = total[4 * r : 4 * r + 4, :]
        loop(WAYS, lambda r: push_or_keep(slab.at[r], slab_in.at[col_group], UPB, row_group * WAYS + r))

    def finish():
        arrived(UPB, slab_in)
        for j in range(WAYS):
            ugrad_ref[0, :, COLS * j : COLS * (j + 1)] = slab_in[j, 0:4, :]
        arrived(DOWN, acc_d)
        total = acc_d[0]
        for i in range(1, WAYS):
            total = total + acc_d[i]
        dgrad_ref[0] = total * factor
        left(UPB, slab.at[pl.ds(0, WAYS - 1)])

        @pl.when(row_group == col_group)
        def _():
            left(DOWN, acc_d.at[pl.ds(0, WAYS - 1)])

        @pl.when(row_group != col_group)
        def _():
            left(DOWN, acc_d)

    @pl.when(first)
    def _():
        squares = lax.fori_loop(
            0, WAYS,
            lambda t, c: c + jnp.sum(jnp.square(own_ref[0, :, tile(t)].astype(F32)), axis=1, keepdims=True),
            jnp.zeros((TOK, 1), F32),
        )
        inverse = lax.rsqrt(squares * (1.0 / WIDTH) + 1e-06)
        inv_ref[0:TOK, :] = jnp.broadcast_to(inverse, (TOK, 128))
        act_ref[0:TOK, :] = jnp.zeros((TOK, RANK), F32)

        def enter(t):
            cols = tile(t)
            v = own_ref[0, :, cols].astype(F32)
            n = (v * inverse * gain_ref[0, :, cols].astype(F32)).astype(BF)
            normed[:, cols] = n
            act_ref[0:TOK, :] += nn(n, down_ref[0, 0, cols, :])

        loop(WAYS, enter)
        act = act_ref[0:TOK, :]
        sq_out[...] = (act * jax.nn.sigmoid(act)).astype(BF)
        all_here()

        def leave(t):
            j = lax.rem(t + p, WAYS)
            cols = tile(j)
            v = own_ref[0, :, cols].astype(F32)
            hid[:, cols] = (v + nn(sq_out[...], up_ref[0, 0, :, cols])).astype(BF)
            loop(WAYS, lambda i: push(hid.at[strip(i), cols], pieces.at[p], ENDS, 1, i * WAYS + j))

        loop(WAYS, leave)
        arrived(ENDS, pieces)
        choose_and_send(COT, cot_in)

        def extras(k):
            t = target(p, k)
            i, j = t // WAYS, lax.rem(t, WAYS)
            push_or_keep(normed.at[strip(i), tile(j)], norm_in.at[p], NORM, t)
            push_or_keep(sq_out.at[strip(i)], sq0_in.at[p], SQ0, t)

        loop(N, extras)

        arrived(BACK, back_in)

        def home(k):
            t = target(p, k)
            bnd_pick[t] = back_in[back_ref[0, t]]
            push_or_keep(bnd_pick.at[t], bnd.at[my_rows, my_cols], BND0, t)

        loop(N, home)

        def home1(k):
            t = target(p, k)
            push(bnd_pick.at[t], ends_ref.at[0, my_rows, my_cols], BND1, 1, t)

        loop(N, home1)
        arrived(SQ1, sq1_in)

        def choose_sq(t):
            sq_pick[t] = sq1_in[back_ref[0, t]]

        loop(N, choose_sq)
        arrived(SQ0, sq0_in)
        partial(part_u, sq0_in, bnd_pick)
        send_up(part_u, UPA, 0)
        partial(part_u1, sq_pick, pieces)
        send_up(part_u1, UPA1, 1)

        arrived(BND0, bnd)
        gsq_ref[0:TOK, :] = jnp.zeros((TOK, RANK), F32)

        def into(t):
            cols = tile(t)
            gsq_ref[0:TOK, :] += nt(bnd[:, cols], up_ref[0, 0, :, cols])

        loop(WAYS, into)
        act2 = act_ref[0:TOK, :]
        _, ga = middle(act2, gsq_ref[0:TOK, :])
        ga_out[...] = ga
        loop(N, lambda k: push_or_keep(ga_out.at[strip(target(p, k) // WAYS)], ga0_in.at[p], GA0, target(p, k)))
        inv2 = inv_ref[0:TOK, 0:1]
        dots = jnp.sum(ga.astype(F32) * act2, axis=1, keepdims=True) * (1.0 / WIDTH)
        pull = inv2 * inv2 * dots

        def out(t):
            cols = tile(t)
            gn = nt(ga_out[...], down_ref[0, 0, cols, :]) * gain_ref[0, :, cols].astype(F32)
            v = own_ref[0, :, cols].astype(F32)
            ends_ref[0, :, cols] = (bnd[:, cols].astype(F32) + inv2 * gn - v * pull).astype(BF)

        loop(WAYS, out)
        finish_up(UPA)
        arrived(NORM, norm_in)
        arrived(GA0, ga0_in)
        partial(part_d, norm_in, ga0_in)
        send_down()
        finish()
        left(ENDS, pieces)
        left(COT, cot_in)
        left(NORM, norm_in.at[pl.ds(0, N - 1)])
        left(SQ0, sq0_in.at[pl.ds(0, N - 1)])
        left(BND0, bnd_pick.at[pl.ds(0, N - 1)])
        left(BND1, bnd_pick)
        left(GA0, ga0_in.at[pl.ds(0, N - 1)])
        left(UPA, acc_u.at[pl.ds(0, WAYS - 1)])
        left(UPA1, acc_u)

    @pl.when(second)
    def _():
        for j in range(WAYS):
            for c in range(COLS // 128):
                at = COLS * j + 128 * c
                gain_out[j, c : c + 1, :] = gain_ref[0, :, at : at + 128].astype(F32)
        all_here()

        def spread(k):
            t = target(p, k)
            push(own_ref.at[0, strip(t // WAYS), tile(lax.rem(t, WAYS))], pieces.at[p], ENDS, 0, t)

        loop(N, spread)

        def gains(k):
            t = target(p, k)
            push_or_keep(gain_out.at[lax.rem(t, WAYS)], gain_in.at[p], GAIN, t)

        loop(N, gains)
        arrived(ENDS, pieces)
        choose_and_send(HID, hid_in)
        arrived(HID, hid_in)

        rows = 2 * TOK
        squares = lax.fori_loop(
            0, WAYS,
            lambda t, c: c + jnp.sum(jnp.square(hid_in[:, :, tile(t)].reshape(rows, COLS).astype(F32)), axis=1, keepdims=True),
            jnp.zeros((rows, 1), F32),
        )
        inverse = lax.rsqrt(squares * (1.0 / WIDTH) + 1e-06)
        act_ref[...] = jnp.zeros((rows, RANK), F32)

        def enter(t):
            cols = tile(t)
            v = hid_in[:, :, cols].reshape(rows, COLS).astype(F32)
            n = (v * inverse * gain_ref[0, :, cols].astype(F32)).astype(BF)
            act_ref[...] += nn(n, down_ref[0, 0, cols, :])

        loop(WAYS, enter)
        arrived(COT, cot_in)
        gsq_ref[...] = jnp.zeros((rows, RANK), F32)

        def into(t):
            cols = tile(t)
            gsq_ref[...] += nt(cot_in[:, :, cols].reshape(rows, COLS), up_ref[0, 0, :, cols])

        loop(WAYS, into)
        act = act_ref[...]
        squashed, ga = middle(act, gsq_ref[...])
        sq_slots[...] = squashed.reshape(2, TOK, RANK)
        ga32 = ga.astype(F32)
        ga_slots[...] = (ga32 * inverse).astype(BF).reshape(2, TOK, RANK)
        dots = jnp.sum(ga32 * act, axis=1, keepdims=True) * (1.0 / WIDTH)
        pull = inverse * inverse * dots

        def out(t):
            j = lax.rem(t + p, WAYS)
            cols = tile(j)
            gn = nt(ga, down_ref[0, 0, cols, :]) * gain_ref[0, :, cols].astype(F32)
            v = hid_in[:, :, cols].reshape(rows, COLS).astype(F32)
            c = cot_in[:, :, cols].reshape(rows, COLS).astype(F32)
            cot_in[:, :, cols] = (c + inverse * gn - v * pull).astype(BF).reshape(2, TOK, COLS)
            loop(
                WAYS,
                lambda i: push(cot_in.at[:, strip(i), cols], back_in.at[pl.ds(2 * p, 2)], BACK, 0, i * WAYS + j),
            )

        loop(WAYS, out)

        def extras(k):
            t = target(p, k)
            at = strip(t // WAYS)
            push(sq_slots.at[:, at], sq1_in.at[pl.ds(2 * p, 2)], SQ1, 0, t)
            push_or_keep(ga_slots.at[:, at], ga1_in.at[pl.ds(2 * p, 2)], GA1, t)

        loop(N, extras)
        arrived(GAIN, gain_in)
        arrived(GA1, ga1_in)

        def choose_ga(t):
            at = back_ref[0, t]
            sq_pick[t] = ga1_in[at]
            g = gain_in[lax.div(at, 2)]
            for c in range(COLS // 128):
                cols = pl.ds(128 * c, 128)
                norm_in[t, :, cols] = (pieces[t, :, cols].astype(F32) * g[c : c + 1, :]).astype(BF)

        loop(N, choose_ga)
        partial(part_d, norm_in, sq_pick)
        send_down()
        finish_up(UPA1)
        finish()
        arrived(BND1, ends_ref.at[0])
        left(ENDS, pieces)
        left(GAIN, gain_in.at[pl.ds(0, N - 1)])
        left(HID, picked.at[pl.ds(0, N - 1)])
        left(BACK, back_in)
        left(SQ1, sq1_in)
        left(GA1, ga1_in.at[pl.ds(0, 2 * N - 2)])


def shards(batch_ends, wiring, down_proj, up_proj, norm_gain):
    ids = jnp.arange(N, dtype=jnp.int32)
    goes = wiring[:, None] == ids[None, :]
    earliest = jnp.min(jnp.where(goes, ids[:, None], N), axis=0)
    latest = jnp.max(jnp.where(goes, ids[:, None], -1), axis=0)
    sources = jnp.stack([jnp.where(earliest == N, 0, earliest), jnp.maximum(latest, 0)])
    again = jnp.any((wiring[:, None] == wiring[None, :]) & (ids[None, :] < ids[:, None]), axis=1)
    slots = (2 * wiring + again.astype(jnp.int32))[None]
    vmem = pl.BlockSpec(memory_space=pltpu.VMEM)
    smem = pl.BlockSpec(memory_space=pltpu.SMEM)
    block = (TOK, WIDTH)
    scratch = [
        pltpu.VMEM((N, ROWS, COLS), BF),
        pltpu.VMEM((N, 2, ROWS, COLS), BF),
        pltpu.VMEM(block, BF),
        pltpu.VMEM(block, BF),
        pltpu.VMEM((2, *block), BF),
        pltpu.VMEM((2, *block), BF),
        pltpu.VMEM((WAYS, 8, 128), F32),
        pltpu.VMEM((N, 8, 128), F32),
        pltpu.VMEM((N, ROWS, COLS), BF),
        pltpu.VMEM((TOK, RANK), BF),
        pltpu.VMEM((N, ROWS, RANK), BF),
        pltpu.VMEM((2, TOK, RANK), BF),
        pltpu.VMEM((2, TOK, RANK), BF),
        pltpu.VMEM((2 * N, ROWS, COLS), BF),
        pltpu.VMEM((2 * N, ROWS, RANK), BF),
        pltpu.VMEM((2 * N, ROWS, RANK), BF),
        pltpu.VMEM((N, ROWS, COLS), BF),
        pltpu.VMEM(block, BF),
        pltpu.VMEM((N, ROWS, RANK), BF),
        pltpu.VMEM((TOK, RANK), BF),
        pltpu.VMEM((N, ROWS, RANK), BF),
        pltpu.VMEM((2 * TOK, RANK), F32),
        pltpu.VMEM((2 * TOK, RANK), F32),
        pltpu.VMEM((TOK, 128), F32),
        pltpu.VMEM((COLS, RANK), F32),
        pltpu.VMEM((RANK, COLS), F32),
        pltpu.VMEM((RANK, COLS), F32),
        pltpu.VMEM((WAYS, 80, RANK), F32),
        pltpu.VMEM((WAYS, 32, COLS), F32),
        pltpu.VMEM((WAYS, 8, COLS), F32),
        pltpu.VMEM((WAYS, 8, COLS), F32),
        pltpu.SemaphoreType.DMA((CLASSES,)),
        pltpu.SemaphoreType.DMA((CLASSES,)),
    ]
    return pl.pallas_call(
        step_kernel,
        out_shape=(
            jax.ShapeDtypeStruct((1, *block), BF),
            jax.ShapeDtypeStruct((1, WIDTH // N, RANK), F32),
            jax.ShapeDtypeStruct((1, RANK // N, WIDTH), F32),
        ),
        in_specs=[smem, smem, vmem, vmem, vmem, vmem],
        out_specs=(vmem, vmem, vmem),
        scratch_shapes=scratch,
        compiler_params=pltpu.CompilerParams(
            collective_id=0, has_side_effects=True, vmem_limit_bytes=56 * 1024 * 1024
        ),
        name="adapter_step",
    )(sources, slots, batch_ends, down_proj, up_proj, norm_gain)


def solution(mesh):
    return jax.shard_map(
        shards,
        mesh=mesh,
        in_specs=(
            P("section", "peer", None),
            P(),
            P("section", "peer", None, None),
            P("section", "peer", None, None),
            P("section", "peer", None),
        ),
        out_specs=(
            P("section", "peer", None),
            P("section", "peer", None),
            P("section", "peer", None),
        ),
        check_vma=False,
    )
```

time: 1410 us -> 233 us (0.17)
  the two profiles are of different devices: /device:TPU:0 before, /device:TPU:73 now
where the time goes in v1:
time: 233 us
  Pallas kernels  225 us (97%)
  local copies, waits for them, and re-layouts  3.77 us (2%)
  other arithmetic  3.41 us (1%)
    pallas_call x1, Pallas kernels, shards(): pl.pallas_call(step_kernel, out_shape=(jax.ShapeDtypeStruct((1, *block),...  225 us

profile of v1, /device:TPU:73, one launch (start us, length us, event | category | flops | bytes accessed | tf_op | source)
XLA Modules:
  0.0 232.9 jit_solution(4665599169240122242)
XLA Ops:
  0.6 0.9 fusion.1
  1.5 1.2 add_bitcast_fusion.back_ref
  2.7 0.7 select_reduce_fusion.1
  3.5 0.6 pad_add_fusion.from_ref
  4.1 225.0 %adapter_step.1 = (bf16[1,128,5120]{2,1,0:T(8,128)(2,1)}, f32[1,80,256]{2,1,0:T(8,128)}, f32[1,4,5120]{2,1,0:T(4,128)}) custom-call(s32[2,64]{1,0:T(2,128)} %pad_add_fusion.from_ref, s32[1,64]{1,0:T(1,128)} %add_bitcast_fusion.back_ref, bf16[1,128,5120]{2,1,0:T(8,128)(2,1)} %own_ref.1, bf16[1,1,5120,256]{3,2,1,0:T(8,128)(2,1)} %down_ref.1, ...), custom_call_target="tpu_custom_call" | custom-call | tf_op jit(solution)/shard_map/adapter_step/pallas_call | solution.py:444
  229.1 0.0 copy-start.1
  229.1 0.0 copy-start
  229.1 2.5 %copy.11 = bf16[1,128,5120]{2,1,0:T(8,128)(2,1)} copy(bf16[1,128,5120]{2,1,0:T(8,128)(2,1)} %get-tuple-element.8) | data formatting | bytes 2621440
  231.6 0.0 copy-done.1
  231.6 0.6 copy.12
  232.2 0.0 copy-done
  232.2 0.6 copy.13
  (2 shorter events, 0.0 us)
Async XLA Ops:
  229.1 2.5 %copy-start.1 = (f32[1,80,256]{2,1,0:T(8,128)S(1)}, f32[1,80,256]{2,1,0:T(8,128)}, u32[]{:S(2)}) copy-start(f32[1,80,256]{2,1,0:T(8,128)} %get-tuple-element.9) | copy-start | bytes 245764
  229.1 3.1 %copy-start = (f32[1,4,5120]{2,1,0:T(4,128)S(1)}, f32[1,4,5120]{2,1,0:T(4,128)}, u32[]{:S(2)}) copy-start(f32[1,4,5120]{2,1,0:T(4,128)} %get-tuple-element.10) | copy-start | bytes 245764

commit v2 on v1

v2 whole, which is shorter than its diff:
```python
import functools
import math

import jax
import jax.numpy as jnp
from jax import lax
from jax.experimental import pallas as pl
from jax.experimental.pallas import tpu as pltpu
from jax.sharding import PartitionSpec as P

N = 64
ROWS = 16
COLS = 640
WAYS = 8
TOK, WIDTH, RANK = 128, 5120, 256
BF, F32 = jnp.bfloat16, jnp.float32
MESH = pl.DeviceIdType.MESH

STAGES = 2
GROUPS = WAYS // STAGES
PART = TOK // STAGES
WIDE = 1280

(ENDS, GAIN, NORM, SQ0, BACK, SQ1, GA1, BND1, GA0, DOWN, DOWN0, UPA, UPA1, UPB) = range(14)
COT, HID, BND0 = 14, 14 + STAGES, 14 + 2 * STAGES
CLASSES = 14 + 3 * STAGES
(OWN, DOWN_W, UP_W, TABLE, LOADS) = range(5)


def target(p, k):
    a = lax.rem(lax.rem(k, 4) + 2 * lax.rem(p, 2), 4)
    b = lax.rem(k // 4, 4)
    x = lax.rem(p // 16 + a, 4)
    y = lax.rem(lax.rem(p // 4, 4) + a + b, 4)
    z = lax.rem(lax.rem(p // 2, 2) + lax.rem(k // 16, 2) + a, 2)
    core = lax.rem(lax.rem(p, 2) + k // 32 + a // 2, 2)
    return x * 16 + y * 4 + z * 2 + core


def place(k):
    m = k // 2
    return lax.rem(k, 2) * GROUPS + m // WAYS, lax.rem(m, WAYS)


def holder(i, j):
    return 2 * (lax.rem(i, GROUPS) * WAYS + j) + i // GROUPS


def mate(p, stage, m):
    a = lax.rem(lax.rem(m, 4) + 2 * lax.rem(p, 2), 4)
    b = lax.rem(m // 4, 4)
    x = lax.rem(p // 16 + a, 4)
    y = lax.rem(lax.rem(p // 4, 4) + a + b, 4)
    z = lax.rem(lax.rem(p // 2, 2) + m // 16 + a, 2)
    return x * 16 + y * 4 + z * 2 + stage


def nn(left, right):
    return jnp.dot(left, right, preferred_element_type=F32)


def nt(left, right):
    return lax.dot_general(left, right, (((1,), (1,)), ((), ())), preferred_element_type=F32)


def tn(left, right):
    return lax.dot_general(left, right, (((0,), (0,)), ((), ())), preferred_element_type=F32)


def loop(count, body):
    def step(k, carry):
        body(k)
        return carry

    lax.fori_loop(0, count, step, 0)


def tile(t):
    return pl.ds(pl.multiple_of(t * COLS, 128), COLS)


def wide(t):
    return pl.ds(pl.multiple_of(t * WIDE, 128), WIDE)


def strip(i):
    return pl.ds(pl.multiple_of(i * ROWS, ROWS), ROWS)


def step_kernel(
    wiring_ref, gain_ref, own_any, down_any, up_any,
    ends_ref, dgrad_ref, ugrad_ref,
    own, down, up, pieces, picked, hid, normed, hid_in, cot_in, gain_out, gain_in, norm_in,
    sq_out, sq0_in, sq_slots, ga_slots, back_in, sq1_in, ga1_in, gathered, bnd, sq_pick,
    ga_out, ga0_in, act_ref, gsq_ref, inv_ref, part_d, part_u, small_d, small_d0, small_u, small_u1,
    acc_d, acc_u, slab, slab_in, table_v, table,
    load, send, recv,
):
    s = lax.axis_index("section")
    p = lax.axis_index("peer")
    first, second = s == 0, s == 1
    my_i, my_j = place(p)
    my_stage = my_i // GROUPS
    my_rows, my_cols = strip(my_i), tile(my_j)

    def push(src, dst, kind, section, peer, out=None):
        pltpu.make_async_remote_copy(
            src_ref=src, dst_ref=dst, send_sem=send.at[kind if out is None else out], recv_sem=recv.at[kind],
            device_id={"section": section, "peer": peer}, device_id_type=MESH,
        ).start()

    def push_or_keep(src, dst, kind, peer, out=None):
        @pl.when(peer != p)
        def _():
            push(src, dst, kind, s, peer, out)

        @pl.when(peer == p)
        def _():
            pltpu.make_async_copy(src, dst, recv.at[kind]).start()

    def arrived(kind, ref):
        pltpu.make_async_copy(ref, ref, recv.at[kind]).wait()

    def left(kind, ref):
        pltpu.make_async_copy(ref, ref, send.at[kind]).wait()

    own_load = pltpu.make_async_copy(own_any.at[0], own, load.at[OWN])
    down_load = pltpu.make_async_copy(down_any.at[0, 0], down, load.at[DOWN_W])
    up_load = pltpu.make_async_copy(up_any.at[0, 0], up, load.at[UP_W])
    table_load = pltpu.make_async_copy(table_v, table, load.at[TABLE])
    own_load.start()
    down_load.start()
    up_load.start()

    barrier = pltpu.get_barrier_semaphore()

    def greet(k):
        t = target(p, k)
        pl.semaphore_signal(barrier, inc=1, device_id={"section": 1 - s, "peer": t}, device_id_type=MESH)

        @pl.when(t != p)
        def _():
            pl.semaphore_signal(barrier, inc=1, device_id={"section": s, "peer": t}, device_id_type=MESH)

    loop(N, greet)

    def all_here():
        pl.semaphore_wait(barrier, 2 * N - 1)

    def make_table():
        lane = lax.broadcasted_iota(jnp.int32, (N, N), 1)
        line = lax.broadcasted_iota(jnp.int32, (N, N), 0)
        wired = jnp.broadcast_to(wiring_ref[...], (N, N))
        goes = wired == line
        earliest = jnp.min(jnp.where(goes, lane, N), axis=1, keepdims=True)
        latest = jnp.max(jnp.where(goes, lane, -1), axis=1, keepdims=True)
        mine = jnp.max(jnp.where(lane == line, wired, 0), axis=1, keepdims=True)
        again = jnp.max(jnp.where((wired == mine) & (lane < line), 1, 0), axis=1, keepdims=True)
        column = lax.broadcasted_iota(jnp.int32, (N, 128), 1)
        table_v[...] = jnp.where(
            column == 0,
            jnp.where(earliest == N, 0, earliest),
            jnp.where(column == 1, jnp.maximum(latest, 0), 2 * mine + again),
        )
        table_load.start()

    def choose_and_send(kind, dst_ref):
        def one(k):
            q = target(p, k)
            picked[q, 0] = pieces[table[q, 0]]
            picked[q, 1] = pieces[table[q, 1]]
            dst = dst_ref.at[:, my_rows, my_cols]
            if kind == HID:
                push_or_keep(picked.at[q], dst, kind + my_stage, q, kind)
            else:
                push(picked.at[q], dst, kind + my_stage, 1, q, kind)

        loop(N, one)

    def middle(act, gsq):
        sig = jax.nn.sigmoid(act)
        squashed = (act * sig).astype(BF)
        ga = (gsq * sig * (1.0 + act * (1.0 - sig))).astype(BF)
        return squashed, ga

    def partial(small, out, left_ref, right_ref):
        out[...] = jnp.zeros_like(out)

        def some(t):
            rows = pl.ds(t * 16, 16)
            a = left_ref[rows].reshape(16 * ROWS, left_ref.shape[2])
            b = right_ref[rows].reshape(16 * ROWS, right_ref.shape[2])
            out[...] += tn(a, b)

        loop(4, some)
        small[...] = out[...].astype(BF)

    def send_up(part, kind):
        def one(i):
            src = part.at[pl.ds(pl.multiple_of(i * 32, 32), 32)]
            dst = acc_u.at[my_i]
            peer = holder(i, my_j)
            if kind == UPA:
                push_or_keep(src, dst, kind, peer)
            else:
                push(src, dst, kind, 1, peer)

        loop(WAYS, one)

    def send_down(part, kind):
        def one(r):
            src = part.at[pl.ds(pl.multiple_of(r * 80, 16), 80)]
            peer = my_j * WAYS + r
            if kind == DOWN:
                push_or_keep(src, acc_d.at[my_i], kind, peer)
            else:
                push(src, acc_d.at[my_i], kind, 0, peer)

        loop(WAYS, one)

    factor = 1.0 / math.sqrt(TOK * N)

    def total_of(acc):
        total = acc[0].astype(F32)
        for i in range(1, WAYS):
            total = total + acc[i].astype(F32)
        return total * factor

    def finish_up(kind):
        arrived(kind, acc_u)
        total = total_of(acc_u)
        for r in range(WAYS):
            slab[r, 0:4, :] = total[4 * r : 4 * r + 4, :]
        loop(WAYS, lambda r: push_or_keep(slab.at[r], slab_in.at[my_j], UPB, my_i * WAYS + r))

    def left_but_own(kind, ref, has_own):
        @pl.when(has_own)
        def _():
            left(kind, ref.at[pl.ds(0, WAYS - 1)])

        @pl.when(jnp.logical_not(has_own))
        def _():
            left(kind, ref)

    def finish(kind):
        arrived(UPB, slab_in)
        for j in range(WAYS):
            ugrad_ref[0, :, COLS * j : COLS * (j + 1)] = slab_in[j, 0:4, :]
        arrived(kind, acc_d)
        dgrad_ref[0] = total_of(acc_d)
        left_but_own(UPB, slab, my_i == p // WAYS)

    @pl.when(first)
    def _():
        own_load.wait()

        def forward(stage):
            rows = pl.ds(pl.multiple_of(stage * PART, PART), PART)
            squares = lax.fori_loop(
                0, WIDTH // WIDE,
                lambda t, c: c + jnp.sum(jnp.square(own[rows, wide(t)].astype(F32)), axis=1, keepdims=True),
                jnp.zeros((PART, 1), F32),
            )
            inverse = lax.rsqrt(squares * (1.0 / WIDTH) + 1e-06)
            inv_ref[rows, :] = jnp.broadcast_to(inverse, (PART, 128))
            act_ref[rows, :] = jnp.zeros((PART, RANK), F32)

            @pl.when(stage == 0)
            def _():
                down_load.wait()

            def enter(t):
                cols = wide(t)
                v = own[rows, cols].astype(F32)
                n = (v * inverse * gain_ref[0, :, cols].astype(F32)).astype(BF)
                normed[rows, cols] = n
                act_ref[rows, :] += nn(n, down[cols, :])

            loop(WIDTH // WIDE, enter)
            act = act_ref[rows, :]
            sq_out[rows, :] = (act * jax.nn.sigmoid(act)).astype(BF)

            @pl.when(stage == 0)
            def _():
                up_load.wait()

            def leave(t):
                cols = wide(t)
                v = own[rows, cols].astype(F32)
                hid[rows, cols] = (v + nn(sq_out[rows, :], up[:, cols])).astype(BF)

            loop(WIDTH // WIDE, leave)

            @pl.when(stage == 0)
            def _():
                all_here()

            def spread(m):
                t = mate(p, stage, m)
                i, j = place(t)
                push(hid.at[strip(i), tile(j)], pieces.at[p], ENDS, 1, t)

            loop(N // STAGES, spread)

        loop(STAGES, forward)
        make_table()
        table_load.wait()
        arrived(ENDS, pieces)
        choose_and_send(COT, cot_in)

        def backward(stage):
            rows = pl.ds(pl.multiple_of(stage * PART, PART), PART)

            @pl.when(stage == my_stage)
            def _():
                arrived(BACK, back_in)

                def home(k):
                    t = target(p, k)
                    gathered[t] = back_in[table[t, 2]]
                    push_or_keep(gathered.at[t], bnd.at[my_rows, my_cols], BND0 + stage, t, BND0)

                loop(N, home)

                def home1(k):
                    t = target(p, k)
                    push(gathered.at[t], ends_ref.at[0, my_rows, my_cols], BND1, 1, t)

                loop(N, home1)

            arrived(BND0 + stage, bnd.at[rows, :])
            gsq_ref[rows, :] = jnp.zeros((PART, RANK), F32)

            def into(t):
                cols = wide(t)
                gsq_ref[rows, :] += nt(bnd[rows, cols], up[:, cols])

            loop(WIDTH // WIDE, into)
            act = act_ref[rows, :]
            _, ga = middle(act, gsq_ref[rows, :])
            ga_out[rows, :] = ga

            def give(m):
                t = mate(p, stage, m)
                i, _ = place(t)
                push(ga_out.at[strip(i)], ga0_in.at[p], GA0, 1, t)

            loop(N // STAGES, give)
            inverse = inv_ref[rows, 0:1]
            dots = jnp.sum(ga.astype(F32) * act, axis=1, keepdims=True) * (1.0 / WIDTH)
            pull = inverse * inverse * dots

            def out(t):
                cols = wide(t)
                gn = nt(ga_out[rows, :], down[cols, :]) * gain_ref[0, :, cols].astype(F32)
                v = own[rows, cols].astype(F32)
                ends_ref[0, rows, cols] = (bnd[rows, cols].astype(F32) + inverse * gn - v * pull).astype(BF)

            loop(WIDTH // WIDE, out)

            @pl.when(stage == 0)
            def _():
                def extras(k):
                    t = target(p, k)
                    i, j = place(t)
                    push(normed.at[strip(i), tile(j)], norm_in.at[p], NORM, 1, t)
                    push_or_keep(sq_out.at[strip(i)], sq0_in.at[p], SQ0, t)

                loop(N, extras)

        loop(STAGES, backward)
        arrived(SQ0, sq0_in)
        partial(small_u, part_u, sq0_in, gathered)
        send_up(small_u, UPA)
        arrived(SQ1, sq1_in)

        def choose_sq(t):
            sq_pick[t] = sq1_in[table[t, 2]]

        loop(N, choose_sq)
        partial(small_u1, part_u, sq_pick, pieces)
        send_up(small_u1, UPA1)
        finish_up(UPA)
        finish(DOWN0)
        left(ENDS, pieces)
        left(COT, cot_in)
        left(NORM, norm_in)
        left(SQ0, sq0_in.at[pl.ds(0, N - 1)])
        left(BND0, gathered.at[pl.ds(0, N - 1)])
        left(BND1, gathered)
        left(GA0, ga0_in)
        left(UPA, acc_u.at[pl.ds(0, WAYS - 1)])
        left(UPA1, acc_u)

    @pl.when(second)
    def _():
        own_load.wait()
        all_here()

        def spread(stage):
            def one(m):
                t = mate(p, stage, m)
                i, j = place(t)
                push(own.at[strip(i), tile(j)], pieces.at[p], ENDS, 0, t)

            loop(N // STAGES, one)

        loop(STAGES, spread)
        make_table()
        for j in range(WAYS):
            for c in range(COLS // 128):
                at = COLS * j + 128 * c
                gain_out[j, c : c + 1, :] = gain_ref[0, :, at : at + 128].astype(F32)
        table_load.wait()
        down_load.wait()
        up_load.wait()
        arrived(ENDS, pieces)
        choose_and_send(HID, hid_in)
        both = 2 * PART

        def through(stage):
            rows = pl.ds(pl.multiple_of(stage * PART, PART), PART)
            arrived(HID + stage, hid_in.at[:, rows, :])
            squares = lax.fori_loop(
                0, WIDTH // WIDE,
                lambda t, c: c
                + jnp.sum(jnp.square(hid_in[:, rows, wide(t)].reshape(both, WIDE).astype(F32)), axis=1, keepdims=True),
                jnp.zeros((both, 1), F32),
            )
            inverse = lax.rsqrt(squares * (1.0 / WIDTH) + 1e-06)
            act_ref[0:both, :] = jnp.zeros((both, RANK), F32)

            def enter(t):
                cols = wide(t)
                v = hid_in[:, rows, cols].reshape(both, WIDE).astype(F32)
                n = (v * inverse * gain_ref[0, :, cols].astype(F32)).astype(BF)
                act_ref[0:both, :] += nn(n, down[cols, :])

            loop(WIDTH // WIDE, enter)
            arrived(COT + stage, cot_in.at[:, rows, :])
            gsq_ref[0:both, :] = jnp.zeros((both, RANK), F32)

            def into(t):
                cols = wide(t)
                gsq_ref[0:both, :] += nt(cot_in[:, rows, cols].reshape(both, WIDE), up[:, cols])

            loop(WIDTH // WIDE, into)
            act = act_ref[0:both, :]
            squashed, ga = middle(act, gsq_ref[0:both, :])
            sq_slots[:, rows, :] = squashed.reshape(2, PART, RANK)
            ga32 = ga.astype(F32)
            ga_slots[:, rows, :] = (ga32 * inverse).astype(BF).reshape(2, PART, RANK)
            dots = jnp.sum(ga32 * act, axis=1, keepdims=True) * (1.0 / WIDTH)
            pull = inverse * inverse * dots

            def out(t):
                u = lax.rem(t + p, WIDTH // WIDE)
                cols = wide(u)
                gn = nt(ga, down[cols, :]) * gain_ref[0, :, cols].astype(F32)
                v = hid_in[:, rows, cols].reshape(both, WIDE).astype(F32)
                c = cot_in[:, rows, cols].reshape(both, WIDE).astype(F32)
                cot_in[:, rows, cols] = (c + inverse * gn - v * pull).astype(BF).reshape(2, PART, WIDE)

                def give(n):
                    i = stage * GROUPS + lax.rem(n, GROUPS)
                    j = u * (WIDE // COLS) + n // GROUPS
                    push(cot_in.at[:, strip(i), tile(j)], back_in.at[pl.ds(2 * p, 2)], BACK, 0, holder(i, j))

                loop(GROUPS * WIDE // COLS, give)

            loop(WIDTH // WIDE, out)

        loop(STAGES, through)

        def extras(k):
            t = target(p, k)
            i, j = place(t)
            push(sq_slots.at[:, strip(i)], sq1_in.at[pl.ds(2 * p, 2)], SQ1, 0, t)
            push_or_keep(ga_slots.at[:, strip(i)], ga1_in.at[pl.ds(2 * p, 2)], GA1, t)
            push_or_keep(gain_out.at[j], gain_in.at[p], GAIN, t)

        loop(N, extras)
        arrived(GAIN, gain_in)
        arrived(GA1, ga1_in)

        def choose_ga(t):
            at = table[t, 2]
            sq_pick[t] = ga1_in[at]
            g = gain_in[lax.div(at, 2)]
            for c in range(COLS // 128):
                cols = pl.ds(128 * c, 128)
                gathered[t, :, cols] = (pieces[t, :, cols].astype(F32) * g[c : c + 1, :]).astype(BF)

        loop(N, choose_ga)
        partial(small_d, part_d, gathered, sq_pick)
        send_down(small_d, DOWN)
        arrived(NORM, norm_in)
        arrived(GA0, ga0_in)
        partial(small_d0, part_d, norm_in, ga0_in)
        send_down(small_d0, DOWN0)
        finish_up(UPA1)
        finish(DOWN)
        arrived(BND1, ends_ref.at[0])
        left(ENDS, pieces)
        left(GAIN, gain_in.at[pl.ds(0, N - 1)])
        left(HID, picked.at[pl.ds(0, N - 1)])
        left(BACK, back_in)
        left(SQ1, sq1_in)
        left(GA1, ga1_in.at[pl.ds(0, 2 * N - 2)])
        left_but_own(DOWN, acc_d, my_j == p // WAYS)
        left(DOWN0, acc_d)


def shards(batch_ends, wiring, down_proj, up_proj, norm_gain):
    vmem = pl.BlockSpec(memory_space=pltpu.VMEM)
    hbm = pl.BlockSpec(memory_space=pl.ANY)
    block = (TOK, WIDTH)
    scratch = [
        pltpu.VMEM(block, BF),
        pltpu.VMEM((WIDTH, RANK), BF),
        pltpu.VMEM((RANK, WIDTH), BF),
        pltpu.VMEM((N, ROWS, COLS), BF),
        pltpu.VMEM((N, 2, ROWS, COLS), BF),
        pltpu.VMEM(block, BF),
        pltpu.VMEM(block, BF),
        pltpu.VMEM((2, *block), BF),
        pltpu.VMEM((2, *block), BF),
        pltpu.VMEM((WAYS, 8, 128), F32),
        pltpu.VMEM((N, 8, 128), F32),
        pltpu.VMEM((N, ROWS, COLS), BF),
        pltpu.VMEM((TOK, RANK), BF),
        pltpu.VMEM((N, ROWS, RANK), BF),
        pltpu.VMEM((2, TOK, RANK), BF),
        pltpu.VMEM((2, TOK, RANK), BF),
        pltpu.VMEM((2 * N, ROWS, COLS), BF),
        pltpu.VMEM((2 * N, ROWS, RANK), BF),
        pltpu.VMEM((2 * N, ROWS, RANK), BF),
        pltpu.VMEM((N, ROWS, COLS), BF),
        pltpu.VMEM(block, BF),
        pltpu.VMEM((N, ROWS, RANK), BF),
        pltpu.VMEM((TOK, RANK), BF),
        pltpu.VMEM((N, ROWS, RANK), BF),
        pltpu.VMEM((2 * TOK, RANK), F32),
        pltpu.VMEM((2 * TOK, RANK), F32),
        pltpu.VMEM((TOK, 128), F32),
        pltpu.VMEM((COLS, RANK), F32),
        pltpu.VMEM((RANK, COLS), F32),
        pltpu.VMEM((COLS, RANK), BF),
        pltpu.VMEM((COLS, RANK), BF),
        pltpu.VMEM((RANK, COLS), BF),
        pltpu.VMEM((RANK, COLS), BF),
        pltpu.VMEM((WAYS, 80, RANK), BF),
        pltpu.VMEM((WAYS, 32, COLS), BF),
        pltpu.VMEM((WAYS, 8, COLS), F32),
        pltpu.VMEM((WAYS, 8, COLS), F32),
        pltpu.VMEM((N, 128), jnp.int32),
        pltpu.SMEM((N, 128), jnp.int32),
        pltpu.SemaphoreType.DMA((LOADS,)),
        pltpu.SemaphoreType.DMA((CLASSES,)),
        pltpu.SemaphoreType.DMA((CLASSES,)),
    ]
    return pl.pallas_call(
        step_kernel,
        out_shape=(
            jax.ShapeDtypeStruct((1, *block), BF),
            jax.ShapeDtypeStruct((1, WIDTH // N, RANK), F32),
            jax.ShapeDtypeStruct((1, RANK // N, WIDTH), F32),
        ),
        in_specs=[vmem, vmem, hbm, hbm, hbm],
        out_specs=(vmem, vmem, vmem),
        scratch_shapes=scratch,
        compiler_params=pltpu.CompilerParams(
            collective_id=0, has_side_effects=True, vmem_limit_bytes=56 * 1024 * 1024
        ),
        name="adapter_step",
    )(wiring[None], norm_gain, batch_ends, down_proj, up_proj)


def solution(mesh):
    return jax.shard_map(
        shards,
        mesh=mesh,
        in_specs=(
            P("section", "peer", None),
            P(),
            P("section", "peer", None, None),
            P("section", "peer", None, None),
            P("section", "peer", None),
        ),
        out_specs=(
            P("section", "peer", None),
            P("section", "peer", None),
            P("section", "peer", None),
        ),
        check_vma=False,
    )
```

time: 233 us -> 202 us (0.87)
  the two profiles are of different devices: /device:TPU:73 before, /device:TPU:35 now
where the time goes in v2:
time: 202 us; the launch traced here: 200 us
  Pallas kernels  195 us (97%)
  local copies, waits for them, and re-layouts  3.77 us (2%)
    pallas_call x1, Pallas kernels, shards(): pl.pallas_call(step_kernel, out_shape=(jax.ShapeDtypeStruct((1, *block),...  195 us

profile of v2, /device:TPU:35, one launch (start us, length us, event | category | flops | bytes accessed | tf_op | source)
XLA Modules:
  0.0 199.6 jit_solution(11838854888769493783)
XLA Ops:
  0.6 195.2 %adapter_step.1 = (bf16[1,128,5120]{2,1,0:T(8,128)(2,1)}, f32[1,80,256]{2,1,0:T(8,128)}, f32[1,4,5120]{2,1,0:T(4,128)}) custom-call(s32[1,64]{1,0:T(1,128)} %bitcast.1, bf16[1,1,5120]{2,1,0:T(2,128)(2,1)} %gain_ref.1, bf16[1,128,5120]{2,1,0:T(8,128)(2,1)} %own_any.1, bf16[1,1,5120,256]{3,2,1,0:T(8,128)(2,1)} %down_any.1, bf16[1,1,256,5120]{3,2,1,0:T(8,128)(2,1)} %up_any.1), custom_call_target="tpu_custom_call" | custom-call | tf_op jit(solution)/shard_map/adapter_step/pallas_call | solution.py:562
  195.8 0.0 copy-start.1
  195.8 0.0 copy-start
  195.9 2.5 %copy.11 = bf16[1,128,5120]{2,1,0:T(8,128)(2,1)} copy(bf16[1,128,5120]{2,1,0:T(8,128)(2,1)} %get-tuple-element.6) | data formatting | bytes 2621440
  198.4 0.0 copy-done.1
  198.4 0.6 copy.12
  199.0 0.0 copy-done
  199.0 0.6 copy.13
Async XLA Ops:
  195.8 2.5 %copy-start.1 = (f32[1,80,256]{2,1,0:T(8,128)S(1)}, f32[1,80,256]{2,1,0:T(8,128)}, u32[]{:S(2)}) copy-start(f32[1,80,256]{2,1,0:T(8,128)} %get-tuple-element.7) | copy-start | bytes 245764
  195.8 3.1 %copy-start = (f32[1,4,5120]{2,1,0:T(4,128)S(1)}, f32[1,4,5120]{2,1,0:T(4,128)}, u32[]{:S(2)}) copy-start(f32[1,4,5120]{2,1,0:T(4,128)} %get-tuple-element.8) | copy-start | bytes 245764

commit v3 on v2

--- a/solution.py
+++ b/solution.py
@@ -21,9 +21,10 @@
 PART = TOK // STAGES
 WIDE = 1280
 
-(ENDS, GAIN, NORM, SQ0, BACK, SQ1, GA1, BND1, GA0, DOWN, DOWN0, UPA, UPA1, UPB) = range(14)
-COT, HID, BND0 = 14, 14 + STAGES, 14 + 2 * STAGES
-CLASSES = 14 + 3 * STAGES
+(ENDS, ENDH, GAIN, NORM, SQ0, COT, COT_LATE, HID, BOTH, BACK, SG, SQF, GAF, BND1, GA0, DOWN, DOWN1, UPA, UPA1, UPB, BND0) = range(21)
+CLASSES = 20 + STAGES
+EARLY = 16
+CHUNK = 128
 (OWN, DOWN_W, UP_W, TABLE, LOADS) = range(5)
 
 
@@ -90,17 +91,18 @@
 def step_kernel(
     wiring_ref, gain_ref, own_any, down_any, up_any,
     ends_ref, dgrad_ref, ugrad_ref,
-    own, down, up, pieces, picked, hid, normed, hid_in, cot_in, gain_out, gain_in, norm_in,
-    sq_out, sq0_in, sq_slots, ga_slots, back_in, sq1_in, ga1_in, gathered, bnd, sq_pick,
-    ga_out, ga0_in, act_ref, gsq_ref, inv_ref, part_d, part_u, small_d, small_d0, small_u, small_u1,
+    own, down, up, pieces, pieces_h, picked, hid, normed, ins, gain_out, gain_in, norm_in, norm1,
+    sq_out, sq0_in, sg_slots, back_in, sg_in, sg_pick, sqf, gaf, gathered, bnd,
+    ga_out, ga0_in, act_ref, gsq_ref, inv_ref, part_d, part_u, small_d, small_d1, small_u, small_u1,
     acc_d, acc_u, slab, slab_in, table_v, table,
-    load, send, recv,
+    load, send, recv, go,
 ):
     s = lax.axis_index("section")
     p = lax.axis_index("peer")
     first, second = s == 0, s == 1
     my_i, my_j = place(p)
     my_stage = my_i // GROUPS
+    early, late = my_stage == 0, my_stage == 1
     my_rows, my_cols = strip(my_i), tile(my_j)
 
     def push(src, dst, kind, section, peer, out=None):
@@ -109,12 +111,15 @@
             device_id={"section": section, "peer": peer}, device_id_type=MESH,
         ).start()
 
-    def push_or_keep(src, dst, kind, peer, out=None):
-        @pl.when(peer != p)
-        def _():
-            push(src, dst, kind, s, peer, out)
-
-        @pl.when(peer == p)
+    def push_or_keep(src, dst, kind, peer, out=None, section=None):
+        there = s if section is None else section
+        here = (peer == p) & (there == s)
+
+        @pl.when(jnp.logical_not(here))
+        def _():
+            push(src, dst, kind, there, peer, out)
+
+        @pl.when(here)
         def _():
             pltpu.make_async_copy(src, dst, recv.at[kind]).start()
 
@@ -164,18 +169,59 @@
         )
         table_load.start()
 
-    def choose_and_send(kind, dst_ref):
-        def one(k):
-            q = target(p, k)
-            picked[q, 0] = pieces[table[q, 0]]
-            picked[q, 1] = pieces[table[q, 1]]
-            dst = dst_ref.at[:, my_rows, my_cols]
-            if kind == HID:
-                push_or_keep(picked.at[q], dst, kind + my_stage, q, kind)
-            else:
-                push(picked.at[q], dst, kind + my_stage, 1, q, kind)
+    def choose(first_slot, source, q):
+        picked[q, first_slot] = source[table[q, 0]]
+        picked[q, first_slot + 1] = source[table[q, 1]]
+
+    def scale():
+        arrived(GAIN, gain_in)
+
+        def one(t):
+            g = gain_in[lax.div(table[t, 2], 2)]
+            for c in range(COLS // 128):
+                cols = pl.ds(128 * c, 128)
+                norm1[t, :, cols] = (pieces_h[t, :, cols].astype(F32) * g[c : c + 1, :]).astype(BF)
 
         loop(N, one)
+
+    def send_home(stage):
+        arrived(BACK, back_in)
+
+        def home(k):
+            t = target(p, k)
+            gathered[t] = back_in[table[t, 2]]
+            push_or_keep(gathered.at[t], bnd.at[my_rows, my_cols], BND0 + stage, t, BND0, section=0)
+
+        loop(N, home)
+
+        @pl.when(lax.rem(my_j, 2) == 0)
+        def _():
+            arrived(SG, sg_in)
+
+            def choose_sg(t):
+                sg_pick[t] = sg_in[table[t, 2]]
+
+            loop(N, choose_sg)
+            c = lax.rem(my_j // 2, 2)
+
+            @pl.when(my_j < 4)
+            def _():
+                loop(WAYS, lambda j: push_or_keep(sg_pick, sqf.at[c], SQF, holder(my_i, j), section=0))
+
+            @pl.when(my_j >= 4)
+            def _():
+                loop(WAYS, lambda j: push(sg_pick, gaf.at[c], GAF, 1 - stage, holder(my_i, j)))
+
+        def home1(k):
+            t = target(p, k)
+            push_or_keep(gathered.at[t], ends_ref.at[0, my_rows, my_cols], BND1, t, section=1)
+
+        loop(N, home1)
+
+    def up0():
+        arrived(SQ0, sq0_in)
+        partial(small_u, part_u, some_rows(sq0_in), some_rows(gathered))
+        send_up(small_u, UPA)
 
     def middle(act, gsq):
         sig = jax.nn.sigmoid(act)
@@ -183,14 +229,21 @@
         ga = (gsq * sig * (1.0 + act * (1.0 - sig))).astype(BF)
         return squashed, ga
 
-    def partial(small, out, left_ref, right_ref):
+    def some_rows(ref):
+        return lambda t: ref[pl.ds(t * 16, 16)].reshape(16 * ROWS, ref.shape[2])
+
+    def some_chunks(ref):
+        def rows(t):
+            at = pl.ds(t * 16, 16)
+            return jnp.concatenate([ref[c, at].reshape(16 * ROWS, CHUNK) for c in range(2)], axis=1)
+
+        return rows
+
+    def partial(small, out, left_of, right_of):
         out[...] = jnp.zeros_like(out)
 
         def some(t):
-            rows = pl.ds(t * 16, 16)
-            a = left_ref[rows].reshape(16 * ROWS, left_ref.shape[2])
-            b = right_ref[rows].reshape(16 * ROWS, right_ref.shape[2])
-            out[...] += tn(a, b)
+            out[...] += tn(left_of(t), right_of(t))
 
         loop(4, some)
         small[...] = out[...].astype(BF)
@@ -201,22 +254,35 @@
             dst = acc_u.at[my_i]
             peer = holder(i, my_j)
             if kind == UPA:
-                push_or_keep(src, dst, kind, peer)
+                push_or_keep(src, dst, kind, peer, section=0)
             else:
                 push(src, dst, kind, 1, peer)
 
         loop(WAYS, one)
 
-    def send_down(part, kind):
+    def send_down(part, kind, section):
         def one(r):
             src = part.at[pl.ds(pl.multiple_of(r * 80, 16), 80)]
-            peer = my_j * WAYS + r
-            if kind == DOWN:
-                push_or_keep(src, acc_d.at[my_i], kind, peer)
-            else:
-                push(src, acc_d.at[my_i], kind, 0, peer)
+            push_or_keep(src, acc_d.at[my_i], kind, my_j * WAYS + r, section=section)
 
         loop(WAYS, one)
+
+    def down1():
+        arrived(GAF, gaf)
+        partial(small_d1, part_d, some_rows(norm1), some_chunks(gaf))
+        send_down(small_d1, DOWN1, 1)
+
+    def left_chunks(sender, count):
+        even = (lax.rem(my_j, 2) == 0) & sender
+        per_chunk = N * ROWS * CHUNK // RANK
+
+        @pl.when(even & (my_j < 4))
+        def _():
+            left(SQF, down.at[pl.ds(0, count * per_chunk)])
+
+        @pl.when(even & (my_j >= 4))
+        def _():
+            left(GAF, down.at[pl.ds(0, WAYS * per_chunk)])
 
     factor = 1.0 / math.sqrt(TOK * N)
 
@@ -255,7 +321,7 @@
         own_load.wait()
 
         def forward(stage):
-            rows = pl.ds(pl.multiple_of(stage * PART, PART), PART)
+            rows = pl.ds(stage * PART, PART)
             squares = lax.fori_loop(
                 0, WIDTH // WIDE,
                 lambda t, c: c + jnp.sum(jnp.square(own[rows, wide(t)].astype(F32)), axis=1, keepdims=True),
@@ -265,8 +331,7 @@
             inv_ref[rows, :] = jnp.broadcast_to(inverse, (PART, 128))
             act_ref[rows, :] = jnp.zeros((PART, RANK), F32)
 
-            @pl.when(stage == 0)
-            def _():
+            if stage == 0:
                 down_load.wait()
 
             def enter(t):
@@ -280,8 +345,7 @@
             act = act_ref[rows, :]
             sq_out[rows, :] = (act * jax.nn.sigmoid(act)).astype(BF)
 
-            @pl.when(stage == 0)
-            def _():
+            if stage == 0:
                 up_load.wait()
 
             def leave(t):
@@ -291,42 +355,84 @@
 
             loop(WIDTH // WIDE, leave)
 
-            @pl.when(stage == 0)
-            def _():
-                all_here()
-
-            def spread(m):
+        def spread(stage):
+            def one(m):
                 t = mate(p, stage, m)
                 i, j = place(t)
-                push(hid.at[strip(i), tile(j)], pieces.at[p], ENDS, 1, t)
-
-            loop(N // STAGES, spread)
-
-        loop(STAGES, forward)
+                push_or_keep(hid.at[strip(i), tile(j)], pieces_h.at[p], ENDH, t, section=1 - stage)
+
+            loop(N // STAGES, one)
+
+        def norms(k):
+            t = target(p, k)
+            i, j = place(t)
+            push_or_keep(normed.at[strip(i), tile(j)], norm_in.at[p], NORM, t)
+
+        def squashes(k):
+            t = target(p, k)
+            i, _ = place(t)
+            push_or_keep(sq_out.at[strip(i)], sq0_in.at[p], SQ0, t, section=i // GROUPS)
+
+        forward(0)
+        all_here()
+        spread(0)
+        forward(1)
+        spread(1)
         make_table()
         table_load.wait()
-        arrived(ENDS, pieces)
-        choose_and_send(COT, cot_in)
+
+        @pl.when(early)
+        def _():
+            arrived(ENDS, pieces)
+
+            def one(k, out):
+                q = target(p, k)
+                choose(0, pieces, q)
+                push(picked.at[q, pl.ds(0, 2)], ins.at[pl.ds(2, 2), my_rows, my_cols], COT, 1, q, out)
+
+            loop(EARLY, lambda k: one(k, COT))
+            loop(N - EARLY, lambda k: one(k + EARLY, COT_LATE))
+            loop(N, squashes)
+            loop(N, norms)
+            left(COT, picked.at[pl.ds(0, EARLY), pl.ds(0, 2)])
+            pl.semaphore_signal(go, inc=1, device_id={"section": 0, "peer": p + 1}, device_id_type=MESH)
+
+        @pl.when(late)
+        def _():
+            loop(N, squashes)
+            pl.semaphore_wait(go, 1)
+            arrived(ENDS, pieces)
+            arrived(ENDH, pieces_h)
+
+            def one(k):
+                q = target(p, k)
+                choose(0, pieces_h, q)
+                choose(2, pieces, q)
+                push(picked.at[q], ins.at[:, my_rows, my_cols], BOTH, 1, q)
+
+            loop(N, one)
+            scale()
+            left(BOTH, picked)
+            loop(N, norms)
+
+        def up1():
+            arrived(SQF, sqf)
+            partial(small_u1, part_u, some_chunks(sqf), some_rows(pieces))
+            send_up(small_u1, UPA1)
 
         def backward(stage):
             rows = pl.ds(pl.multiple_of(stage * PART, PART), PART)
 
-            @pl.when(stage == my_stage)
+            @pl.when((stage == 0) & early)
             def _():
-                arrived(BACK, back_in)
-
-                def home(k):
-                    t = target(p, k)
-                    gathered[t] = back_in[table[t, 2]]
-                    push_or_keep(gathered.at[t], bnd.at[my_rows, my_cols], BND0 + stage, t, BND0)
-
-                loop(N, home)
-
-                def home1(k):
-                    t = target(p, k)
-                    push(gathered.at[t], ends_ref.at[0, my_rows, my_cols], BND1, 1, t)
-
-                loop(N, home1)
+                send_home(0)
+
+            @pl.when(stage == 1)
+            def _():
+                @pl.when(early)
+                def _():
+                    up0()
+                    up1()
 
             arrived(BND0 + stage, bnd.at[rows, :])
             gsq_ref[rows, :] = jnp.zeros((PART, RANK), F32)
@@ -343,7 +449,7 @@
             def give(m):
                 t = mate(p, stage, m)
                 i, _ = place(t)
-                push(ga_out.at[strip(i)], ga0_in.at[p], GA0, 1, t)
+                push_or_keep(ga_out.at[strip(i)], ga0_in.at[p], GA0, t)
 
             loop(N // STAGES, give)
             inverse = inv_ref[rows, 0:1]
@@ -358,39 +464,40 @@
 
             loop(WIDTH // WIDE, out)
 
-            @pl.when(stage == 0)
-            def _():
-                def extras(k):
-                    t = target(p, k)
-                    i, j = place(t)
-                    push(normed.at[strip(i), tile(j)], norm_in.at[p], NORM, 1, t)
-                    push_or_keep(sq_out.at[strip(i)], sq0_in.at[p], SQ0, t)
-
-                loop(N, extras)
-
         loop(STAGES, backward)
-        arrived(SQ0, sq0_in)
-        partial(small_u, part_u, sq0_in, gathered)
-        send_up(small_u, UPA)
-        arrived(SQ1, sq1_in)
-
-        def choose_sq(t):
-            sq_pick[t] = sq1_in[table[t, 2]]
-
-        loop(N, choose_sq)
-        partial(small_u1, part_u, sq_pick, pieces)
-        send_up(small_u1, UPA1)
+
+        @pl.when(late)
+        def _():
+            up1()
+            down1()
+
+        arrived(NORM, norm_in)
+        arrived(GA0, ga0_in)
+        partial(small_d, part_d, some_rows(norm_in), some_rows(ga0_in))
+        send_down(small_d, DOWN, 0)
         finish_up(UPA)
-        finish(DOWN0)
-        left(ENDS, pieces)
-        left(COT, cot_in)
-        left(NORM, norm_in)
-        left(SQ0, sq0_in.at[pl.ds(0, N - 1)])
-        left(BND0, gathered.at[pl.ds(0, N - 1)])
-        left(BND1, gathered)
-        left(GA0, ga0_in)
-        left(UPA, acc_u.at[pl.ds(0, WAYS - 1)])
+        finish(DOWN)
+        left_but_own(DOWN, acc_d, my_j == p // WAYS)
+        left(NORM, norm_in.at[pl.ds(0, N - 1)])
+        left(GA0, ga0_in.at[pl.ds(0, N - 1)])
         left(UPA1, acc_u)
+
+        @pl.when(early)
+        def _():
+            left(ENDH, pieces_h)
+            left(SQ0, sq0_in.at[pl.ds(0, N - 1)])
+            left(BND0, gathered.at[pl.ds(0, N - 1)])
+            left(BND1, gathered)
+            left(UPA, acc_u.at[pl.ds(0, WAYS - 1)])
+            left(COT_LATE, picked.at[pl.ds(0, N - EARLY), pl.ds(0, 2)])
+
+        @pl.when(late)
+        def _():
+            left(ENDH, pieces_h.at[pl.ds(0, N - 1)])
+            left(SQ0, sq0_in)
+            left(DOWN1, acc_d)
+
+        left_chunks(early, WAYS - 1)
 
     @pl.when(second)
     def _():
@@ -406,25 +513,54 @@
             loop(N // STAGES, one)
 
         loop(STAGES, spread)
-        make_table()
         for j in range(WAYS):
             for c in range(COLS // 128):
                 at = COLS * j + 128 * c
                 gain_out[j, c : c + 1, :] = gain_ref[0, :, at : at + 128].astype(F32)
-        table_load.wait()
+
+        def gains(k):
+            t = target(p, k)
+            i, j = place(t)
+            push_or_keep(gain_out.at[j], gain_in.at[p], GAIN, t, section=1 - i // GROUPS)
+
+        loop(N, gains)
         down_load.wait()
         up_load.wait()
-        arrived(ENDS, pieces)
-        choose_and_send(HID, hid_in)
+        make_table()
+        table_load.wait()
+
+        @pl.when(early)
+        def _():
+            arrived(ENDH, pieces_h)
+
+            def one(k):
+                q = target(p, k)
+                choose(0, pieces_h, q)
+                push_or_keep(
+                    picked.at[q, pl.ds(0, 2)], ins.at[pl.ds(0, 2), my_rows, my_cols], HID, q
+                )
+
+            loop(N, one)
+            scale()
+
         both = 2 * PART
 
         def through(stage):
             rows = pl.ds(pl.multiple_of(stage * PART, PART), PART)
-            arrived(HID + stage, hid_in.at[:, rows, :])
+
+            @pl.when(stage == 0)
+            def _():
+                arrived(HID, ins.at[pl.ds(0, 2), rows, :])
+                arrived(COT, ins.at[pl.ds(2, 2), rows, :])
+
+            @pl.when(stage == 1)
+            def _():
+                arrived(BOTH, ins.at[:, rows, :])
+
             squares = lax.fori_loop(
                 0, WIDTH // WIDE,
                 lambda t, c: c
-                + jnp.sum(jnp.square(hid_in[:, rows, wide(t)].reshape(both, WIDE).astype(F32)), axis=1, keepdims=True),
+                + jnp.sum(jnp.square(ins[0:2, rows, wide(t)].reshape(both, WIDE).astype(F32)), axis=1, keepdims=True),
                 jnp.zeros((both, 1), F32),
             )
             inverse = lax.rsqrt(squares * (1.0 / WIDTH) + 1e-06)
@@ -432,24 +568,23 @@
 
             def enter(t):
                 cols = wide(t)
-                v = hid_in[:, rows, cols].reshape(both, WIDE).astype(F32)
+                v = ins[0:2, rows, cols].reshape(both, WIDE).astype(F32)
                 n = (v * inverse * gain_ref[0, :, cols].astype(F32)).astype(BF)
                 act_ref[0:both, :] += nn(n, down[cols, :])
 
             loop(WIDTH // WIDE, enter)
-            arrived(COT + stage, cot_in.at[:, rows, :])
             gsq_ref[0:both, :] = jnp.zeros((both, RANK), F32)
 
             def into(t):
                 cols = wide(t)
-                gsq_ref[0:both, :] += nt(cot_in[:, rows, cols].reshape(both, WIDE), up[:, cols])
+                gsq_ref[0:both, :] += nt(ins[2:4, rows, cols].reshape(both, WIDE), up[:, cols])
 
             loop(WIDTH // WIDE, into)
             act = act_ref[0:both, :]
             squashed, ga = middle(act, gsq_ref[0:both, :])
-            sq_slots[:, rows, :] = squashed.reshape(2, PART, RANK)
+            sg_slots[:, rows, 0:RANK] = squashed.reshape(2, PART, RANK)
             ga32 = ga.astype(F32)
-            ga_slots[:, rows, :] = (ga32 * inverse).astype(BF).reshape(2, PART, RANK)
+            sg_slots[:, rows, RANK : 2 * RANK] = (ga32 * inverse).astype(BF).reshape(2, PART, RANK)
             dots = jnp.sum(ga32 * act, axis=1, keepdims=True) * (1.0 / WIDTH)
             pull = inverse * inverse * dots
 
@@ -457,58 +592,67 @@
                 u = lax.rem(t + p, WIDTH // WIDE)
                 cols = wide(u)
                 gn = nt(ga, down[cols, :]) * gain_ref[0, :, cols].astype(F32)
-                v = hid_in[:, rows, cols].reshape(both, WIDE).astype(F32)
-                c = cot_in[:, rows, cols].reshape(both, WIDE).astype(F32)
-                cot_in[:, rows, cols] = (c + inverse * gn - v * pull).astype(BF).reshape(2, PART, WIDE)
+                v = ins[0:2, rows, cols].reshape(both, WIDE).astype(F32)
+                c = ins[2:4, rows, cols].reshape(both, WIDE).astype(F32)
+                ins[2:4, rows, cols] = (c + inverse * gn - v * pull).astype(BF).reshape(2, PART, WIDE)
 
                 def give(n):
                     i = stage * GROUPS + lax.rem(n, GROUPS)
                     j = u * (WIDE // COLS) + n // GROUPS
-                    push(cot_in.at[:, strip(i), tile(j)], back_in.at[pl.ds(2 * p, 2)], BACK, 0, holder(i, j))
+                    push_or_keep(ins.at[pl.ds(2, 2), strip(i), tile(j)], back_in.at[pl.ds(2 * p, 2)], BACK, holder(i, j), section=stage)
 
                 loop(GROUPS * WIDE // COLS, give)
 
             loop(WIDTH // WIDE, out)
 
+            def extras(m):
+                i = stage * GROUPS + lax.rem(m, GROUPS)
+                c = m // GROUPS
+                cols = pl.ds(pl.multiple_of(c * CHUNK, CHUNK), CHUNK)
+                push_or_keep(sg_slots.at[:, strip(i), cols], sg_in.at[pl.ds(2 * p, 2)], SG, holder(i, 2 * c), section=stage)
+
+            loop(GROUPS * (2 * RANK // CHUNK), extras)
+
         loop(STAGES, through)
 
-        def extras(k):
-            t = target(p, k)
-            i, j = place(t)
-            push(sq_slots.at[:, strip(i)], sq1_in.at[pl.ds(2 * p, 2)], SQ1, 0, t)
-            push_or_keep(ga_slots.at[:, strip(i)], ga1_in.at[pl.ds(2 * p, 2)], GA1, t)
-            push_or_keep(gain_out.at[j], gain_in.at[p], GAIN, t)
-
-        loop(N, extras)
-        arrived(GAIN, gain_in)
-        arrived(GA1, ga1_in)
-
-        def choose_ga(t):
-            at = table[t, 2]
-            sq_pick[t] = ga1_in[at]
-            g = gain_in[lax.div(at, 2)]
-            for c in range(COLS // 128):
-                cols = pl.ds(128 * c, 128)
-                gathered[t, :, cols] = (pieces[t, :, cols].astype(F32) * g[c : c + 1, :]).astype(BF)
-
-        loop(N, choose_ga)
-        partial(small_d, part_d, gathered, sq_pick)
-        send_down(small_d, DOWN)
-        arrived(NORM, norm_in)
-        arrived(GA0, ga0_in)
-        partial(small_d0, part_d, norm_in, ga0_in)
-        send_down(small_d0, DOWN0)
+        @pl.when(late)
+        def _():
+            send_home(1)
+            up0()
+
+        pl.when(early)(down1)
         finish_up(UPA1)
-        finish(DOWN)
+        finish(DOWN1)
         arrived(BND1, ends_ref.at[0])
         left(ENDS, pieces)
-        left(GAIN, gain_in.at[pl.ds(0, N - 1)])
-        left(HID, picked.at[pl.ds(0, N - 1)])
-        left(BACK, back_in)
-        left(SQ1, sq1_in)
-        left(GA1, ga1_in.at[pl.ds(0, 2 * N - 2)])
-        left_but_own(DOWN, acc_d, my_j == p // WAYS)
-        left(DOWN0, acc_d)
+
+        @pl.when(early)
+        def _():
+            left(GAIN, gain_in.at[pl.ds(0, N - 1)])
+            left(BACK, back_in)
+            left(HID, picked.at[pl.ds(0, N - 1), pl.ds(0, 2)])
+            left_but_own(DOWN1, acc_d, my_j == p // WAYS)
+
+        @pl.when(late)
+        def _():
+            left(GAIN, gain_in)
+            left(BACK, back_in.at[pl.ds(0, 2 * N - 2)])
+            left(BND0, gathered)
+            left(BND1, gathered.at[pl.ds(0, N - 1)])
+            left(UPA, acc_u)
+
+        own_chunk = late & (lax.rem(my_j, 2) == 0)
+
+        @pl.when(own_chunk)
+        def _():
+            left(SG, sg_in.at[pl.ds(0, N - 2)])
+
+        @pl.when(jnp.logical_not(own_chunk))
+        def _():
+            left(SG, sg_in.at[pl.ds(0, N)])
+
+
+        left_chunks(late, WAYS)
 
 
 def shards(batch_ends, wiring, down_proj, up_proj, norm_gain):
@@ -520,24 +664,25 @@
         pltpu.VMEM((WIDTH, RANK), BF),
         pltpu.VMEM((RANK, WIDTH), BF),
         pltpu.VMEM((N, ROWS, COLS), BF),
-        pltpu.VMEM((N, 2, ROWS, COLS), BF),
+        pltpu.VMEM((N, ROWS, COLS), BF),
+        pltpu.VMEM((N, 4, ROWS, COLS), BF),
         pltpu.VMEM(block, BF),
         pltpu.VMEM(block, BF),
-        pltpu.VMEM((2, *block), BF),
-        pltpu.VMEM((2, *block), BF),
+        pltpu.VMEM((4, *block), BF),
         pltpu.VMEM((WAYS, 8, 128), F32),
         pltpu.VMEM((N, 8, 128), F32),
         pltpu.VMEM((N, ROWS, COLS), BF),
+        pltpu.VMEM((N, ROWS, COLS), BF),
         pltpu.VMEM((TOK, RANK), BF),
         pltpu.VMEM((N, ROWS, RANK), BF),
-        pltpu.VMEM((2, TOK, RANK), BF),
-        pltpu.VMEM((2, TOK, RANK), BF),
+        pltpu.VMEM((2, TOK, 2 * RANK), BF),
         pltpu.VMEM((2 * N, ROWS, COLS), BF),
-        pltpu.VMEM((2 * N, ROWS, RANK), BF),
-        pltpu.VMEM((2 * N, ROWS, RANK), BF),
+        pltpu.VMEM((2 * N, ROWS, CHUNK), BF),
+        pltpu.VMEM((N, ROWS, CHUNK), BF),
+        pltpu.VMEM((2, N, ROWS, CHUNK), BF),
+        pltpu.VMEM((2, N, ROWS, CHUNK), BF),
         pltpu.VMEM((N, ROWS, COLS), BF),
         pltpu.VMEM(block, BF),
-        pltpu.VMEM((N, ROWS, RANK), BF),
         pltpu.VMEM((TOK, RANK), BF),
         pltpu.VMEM((N, ROWS, RANK), BF),
         pltpu.VMEM((2 * TOK, RANK), F32),
@@ -558,6 +703,7 @@
         pltpu.SemaphoreType.DMA((LOADS,)),
         pltpu.SemaphoreType.DMA((CLASSES,)),
         pltpu.SemaphoreType.DMA((CLASSES,)),
+        pltpu.SemaphoreType.REGULAR,
     ]
     return pl.pallas_call(
         step_kernel,

time: 202 us -> 190 us (0.941)
  the two profiles are of different devices: /device:TPU:35 before, /device:TPU:29 now
where the time goes in v3:
time: 190 us
  Pallas kernels  185 us (97%)
  local copies, waits for them, and re-layouts  3.77 us (2%)
    pallas_call x1, Pallas kernels, shards(): pl.pallas_call(step_kernel, out_shape=(jax.ShapeDtypeStruct((1, *block),...  185 us

profile of v3, /device:TPU:29, one launch (start us, length us, event | category | flops | bytes accessed | tf_op | source)
XLA Modules:
  0.0 189.7 jit_solution(12363344177670764720)
XLA Ops:
  0.6 185.3 %adapter_step.1 = (bf16[1,128,5120]{2,1,0:T(8,128)(2,1)}, f32[1,80,256]{2,1,0:T(8,128)}, f32[1,4,5120]{2,1,0:T(4,128)}) custom-call(s32[1,64]{1,0:T(1,128)} %bitcast.1, bf16[1,1,5120]{2,1,0:T(2,128)(2,1)} %gain_ref.1, bf16[1,128,5120]{2,1,0:T(8,128)(2,1)} %own_any.1, bf16[1,1,5120,256]{3,2,1,0:T(8,128)(2,1)} %down_any.1, bf16[1,1,256,5120]{3,2,1,0:T(8,128)(2,1)} %up_any.1), custom_call_target="tpu_custom_call" | custom-call | tf_op jit(solution)/shard_map/adapter_step/pallas_call | solution.py:708
  185.9 0.0 copy-start.1
  185.9 0.0 copy-start
  186.0 2.5 %copy.11 = bf16[1,128,5120]{2,1,0:T(8,128)(2,1)} copy(bf16[1,128,5120]{2,1,0:T(8,128)(2,1)} %get-tuple-element.6) | data formatting | bytes 2621440
  188.4 0.0 copy-done.1
  188.4 0.6 copy.12
  189.1 0.0 copy-done
  189.1 0.6 copy.13
Async XLA Ops:
  185.9 2.5 %copy-start.1 = (f32[1,80,256]{2,1,0:T(8,128)S(1)}, f32[1,80,256]{2,1,0:T(8,128)}, u32[]{:S(2)}) copy-start(f32[1,80,256]{2,1,0:T(8,128)} %get-tuple-element.7) | copy-start | bytes 245764
  185.9 3.1 %copy-start = (f32[1,4,5120]{2,1,0:T(4,128)S(1)}, f32[1,4,5120]{2,1,0:T(4,128)}, u32[]{:S(2)}) copy-start(f32[1,4,5120]{2,1,0:T(4,128)} %get-tuple-element.8) | copy-start | bytes 245764

commit v4 on v3

--- a/solution.py
+++ b/solution.py
@@ -140,14 +140,13 @@
     barrier = pltpu.get_barrier_semaphore()
 
     def greet(k):
-        t = target(p, k)
-        pl.semaphore_signal(barrier, inc=1, device_id={"section": 1 - s, "peer": t}, device_id_type=MESH)
-
-        @pl.when(t != p)
-        def _():
-            pl.semaphore_signal(barrier, inc=1, device_id={"section": s, "peer": t}, device_id_type=MESH)
-
-    loop(N, greet)
+        for n in range(7):
+            t = lax.rem(p + 1 + 7 * k + n, N)
+            for section in (0, 1):
+                pl.semaphore_signal(barrier, inc=1, device_id={"section": section, "peer": t}, device_id_type=MESH)
+
+    loop(9, greet)
+    pl.semaphore_signal(barrier, inc=1, device_id={"section": 1 - s, "peer": p}, device_id_type=MESH)
 
     def all_here():
         pl.semaphore_wait(barrier, 2 * N - 1)
@@ -394,8 +393,8 @@
             loop(N - EARLY, lambda k: one(k + EARLY, COT_LATE))
             loop(N, squashes)
             loop(N, norms)
+            pl.semaphore_signal(go, inc=1, device_id={"section": 0, "peer": p + 1}, device_id_type=MESH)
             left(COT, picked.at[pl.ds(0, EARLY), pl.ds(0, 2)])
-            pl.semaphore_signal(go, inc=1, device_id={"section": 0, "peer": p + 1}, device_id_type=MESH)
 
         @pl.when(late)
         def _():
@@ -466,16 +465,17 @@
 
         loop(STAGES, backward)
 
-        @pl.when(late)
-        def _():
-            up1()
-            down1()
-
         arrived(NORM, norm_in)
         arrived(GA0, ga0_in)
         partial(small_d, part_d, some_rows(norm_in), some_rows(ga0_in))
         send_down(small_d, DOWN, 0)
         finish_up(UPA)
+
+        @pl.when(late)
+        def _():
+            up1()
+            down1()
+
         finish(DOWN)
         left_but_own(DOWN, acc_d, my_j == p // WAYS)
         left(NORM, norm_in.at[pl.ds(0, N - 1)])
@@ -589,7 +589,7 @@
             pull = inverse * inverse * dots
 
             def out(t):
-                u = lax.rem(t + p, WIDTH // WIDE)
+                u = lax.rem(t + p + p // 4 + p // 16, WIDTH // WIDE)
                 cols = wide(u)
                 gn = nt(ga, down[cols, :]) * gain_ref[0, :, cols].astype(F32)
                 v = ins[0:2, rows, cols].reshape(both, WIDE).astype(F32)

time: 190 us -> 181 us (0.953)
  the two profiles are of different devices: /device:TPU:29 before, /device:TPU:35 now
where the time goes in v4:
time: 181 us
  Pallas kernels  177 us (98%)
  local copies, waits for them, and re-layouts  3.77 us (2%)
    pallas_call x1, Pallas kernels, shards(): pl.pallas_call(step_kernel, out_shape=(jax.ShapeDtypeStruct((1, *block),...  177 us
    unnamed x7, local copies, waits for them, and re-layouts  3.77 us

profile of v4, /device:TPU:35, one launch (start us, length us, event | category | flops | bytes accessed | tf_op | source)
XLA Modules:
  0.0 181.3 jit_solution(10511805936202841124)
XLA Ops:
  0.6 176.9 %adapter_step.1 = (bf16[1,128,5120]{2,1,0:T(8,128)(2,1)}, f32[1,80,256]{2,1,0:T(8,128)}, f32[1,4,5120]{2,1,0:T(4,128)}) custom-call(s32[1,64]{1,0:T(1,128)} %bitcast.1, bf16[1,1,5120]{2,1,0:T(2,128)(2,1)} %gain_ref.1, bf16[1,128,5120]{2,1,0:T(8,128)(2,1)} %own_any.1, bf16[1,1,5120,256]{3,2,1,0:T(8,128)(2,1)} %down_any.1, bf16[1,1,256,5120]{3,2,1,0:T(8,128)(2,1)} %up_any.1), custom_call_target="tpu_custom_call" | custom-call | tf_op jit(solution)/shard_map/adapter_step/pallas_call | solution.py:708
  177.5 0.0 copy-start.1
  177.5 0.0 copy-start
  177.5 2.5 %copy.11 = bf16[1,128,5120]{2,1,0:T(8,128)(2,1)} copy(bf16[1,128,5120]{2,1,0:T(8,128)(2,1)} %get-tuple-element.6) | data formatting | bytes 2621440
  180.0 0.0 copy-done.1
  180.0 0.6 copy.12
  180.6 0.0 copy-done
  180.6 0.6 copy.13
Async XLA Ops:
  177.5 2.5 %copy-start.1 = (f32[1,80,256]{2,1,0:T(8,128)S(1)}, f32[1,80,256]{2,1,0:T(8,128)}, u32[]{:S(2)}) copy-start(f32[1,80,256]{2,1,0:T(8,128)} %get-tuple-element.7) | copy-start | bytes 245764
  177.5 3.1 %copy-start = (f32[1,4,5120]{2,1,0:T(4,128)S(1)}, f32[1,4,5120]{2,1,0:T(4,128)}, u32[]{:S(2)}) copy-start(f32[1,4,5120]{2,1,0:T(4,128)} %get-tuple-element.8) | copy-start | bytes 245764

commit v5 on v4

--- a/solution.py
+++ b/solution.py
@@ -25,7 +25,8 @@
 CLASSES = 20 + STAGES
 EARLY = 16
 CHUNK = 128
-(OWN, DOWN_W, UP_W, TABLE, LOADS) = range(5)
+(OWN, DOWN_W, UP_W, TABLE, ENDS_OUT) = range(5)
+LOADS = ENDS_OUT + STAGES
 
 
 def target(p, k):
@@ -92,7 +93,7 @@
     wiring_ref, gain_ref, own_any, down_any, up_any,
     ends_ref, dgrad_ref, ugrad_ref,
     own, down, up, pieces, pieces_h, picked, hid, normed, ins, gain_out, gain_in, norm_in, norm1,
-    sq_out, sq0_in, sg_slots, back_in, sg_in, sg_pick, sqf, gaf, gathered, bnd,
+    sq_out, sq0_in, sg_slots, back_in, sg_in, sg_pick, sqf, gaf, gathered, bnd, ends_v,
     ga_out, ga0_in, act_ref, gsq_ref, inv_ref, part_d, part_u, small_d, small_d1, small_u, small_u1,
     acc_d, acc_u, slab, slab_in, table_v, table,
     load, send, recv, go,
@@ -215,6 +216,8 @@
             t = target(p, k)
             push_or_keep(gathered.at[t], ends_ref.at[0, my_rows, my_cols], BND1, t, section=1)
 
+        if stage == 1:
+            up0()
         loop(N, home1)
 
     def up0():
@@ -459,9 +462,10 @@
                 cols = wide(t)
                 gn = nt(ga_out[rows, :], down[cols, :]) * gain_ref[0, :, cols].astype(F32)
                 v = own[rows, cols].astype(F32)
-                ends_ref[0, rows, cols] = (bnd[rows, cols].astype(F32) + inverse * gn - v * pull).astype(BF)
+                ends_v[rows, cols] = (bnd[rows, cols].astype(F32) + inverse * gn - v * pull).astype(BF)
 
             loop(WIDTH // WIDE, out)
+            pltpu.make_async_copy(ends_v.at[rows, :], ends_ref.at[0, rows, :], load.at[ENDS_OUT + stage]).start()
 
         loop(STAGES, backward)
 
@@ -477,6 +481,9 @@
             down1()
 
         finish(DOWN)
+        for stage in range(STAGES):
+            half = pl.ds(stage * PART, PART)
+            pltpu.make_async_copy(ends_v.at[half, :], ends_ref.at[0, half, :], load.at[ENDS_OUT + stage]).wait()
         left_but_own(DOWN, acc_d, my_j == p // WAYS)
         left(NORM, norm_in.at[pl.ds(0, N - 1)])
         left(GA0, ga0_in.at[pl.ds(0, N - 1)])
@@ -618,7 +625,6 @@
         @pl.when(late)
         def _():
             send_home(1)
-            up0()
 
         pl.when(early)(down1)
         finish_up(UPA1)
@@ -682,6 +688,7 @@
         pltpu.VMEM((2, N, ROWS, CHUNK), BF),
         pltpu.VMEM((2, N, ROWS, CHUNK), BF),
         pltpu.VMEM((N, ROWS, COLS), BF),
+        pltpu.VMEM(block, BF),
         pltpu.VMEM(block, BF),
         pltpu.VMEM((TOK, RANK), BF),
         pltpu.VMEM((N, ROWS, RANK), BF),
@@ -713,7 +720,7 @@
             jax.ShapeDtypeStruct((1, RANK // N, WIDTH), F32),
         ),
         in_specs=[vmem, vmem, hbm, hbm, hbm],
-        out_specs=(vmem, vmem, vmem),
+        out_specs=(hbm, vmem, vmem),
         scratch_shapes=scratch,
         compiler_params=pltpu.CompilerParams(
             collective_id=0, has_side_effects=True, vmem_limit_bytes=56 * 1024 * 1024

time: 181 us -> 180 us (level)
  Pallas kernels: 177 us -> 175 us
where the time goes in v5:
time: 180 us
  Pallas kernels  175 us (97%)
  local copies, waits for them, and re-layouts  3.77 us (2%)
    pallas_call x1, Pallas kernels, shards(): pl.pallas_call(step_kernel, out_shape=(jax.ShapeDtypeStruct((1, *block),...  175 us
    unnamed x7, local copies, waits for them, and re-layouts  3.77 us

profile of v5, /device:TPU:35, one launch (start us, length us, event | category | flops | bytes accessed | tf_op | source)
XLA Modules:
  0.0 179.9 jit_solution(14456448407592016256)
XLA Ops:
  0.6 175.4 %adapter_step.1 = (bf16[1,128,5120]{2,1,0:T(8,128)(2,1)}, f32[1,80,256]{2,1,0:T(8,128)}, f32[1,4,5120]{2,1,0:T(4,128)}) custom-call(s32[1,64]{1,0:T(1,128)} %bitcast.1, bf16[1,1,5120]{2,1,0:T(2,128)(2,1)} %gain_ref.1, bf16[1,128,5120]{2,1,0:T(8,128)(2,1)} %own_any.1, bf16[1,1,5120,256]{3,2,1,0:T(8,128)(2,1)} %down_any.1, bf16[1,1,256,5120]{3,2,1,0:T(8,128)(2,1)} %up_any.1), custom_call_target="tpu_custom_call" | custom-call | tf_op jit(solution)/shard_map/adapter_step/pallas_call | solution.py:715
  176.1 0.0 copy-start.1
  176.1 0.0 copy-start
  176.1 2.5 %copy.11 = bf16[1,128,5120]{2,1,0:T(8,128)(2,1)} copy(bf16[1,128,5120]{2,1,0:T(8,128)(2,1)} %get-tuple-element.6) | data formatting | bytes 2621440
  178.6 0.0 copy-done.1
  178.6 0.6 copy.12
  179.2 0.0 copy-done
  179.2 0.6 copy.13
Async XLA Ops:
  176.1 2.5 %copy-start.1 = (f32[1,80,256]{2,1,0:T(8,128)S(1)}, f32[1,80,256]{2,1,0:T(8,128)}, u32[]{:S(2)}) copy-start(f32[1,80,256]{2,1,0:T(8,128)} %get-tuple-element.7) | copy-start | bytes 245764
  176.1 3.1 %copy-start = (f32[1,4,5120]{2,1,0:T(4,128)S(1)}, f32[1,4,5120]{2,1,0:T(4,128)}, u32[]{:S(2)}) copy-start(f32[1,4,5120]{2,1,0:T(4,128)} %get-tuple-element.8) | copy-start | bytes 245764
